TPU v7x, 32 devices: a whole 2x2x4 slice. The times are simulated.
32 devices in a mesh: dp: 8 (over z, y), mp: 4 (over x, core).
Axes of the slice: x: 2, y: 2, z: 4, core: 2. Of those that a mesh axis runs over, the one named last changes fastest.
Arguments:
- tokens: bfloat16 [8192, 768], P(('dp', 'mp')), may hold values from -6 to 6
- cotangent: bfloat16 [8192, 768], P(('dp', 'mp')), may hold values from -6 to 6
- gain_attn: float32 [768], replicated, may hold values from 0.5 to 1.5
- w_qkv: bfloat16 [3, 768, 768], P(None, 'dp', 'mp'), may hold values from -0.109375 to 0.109375
- w_attn_out: bfloat16 [768, 768], P('mp', 'dp'), may hold values from -1.75 to 1.75
- rel_table: float32 [12, 32], replicated, may hold values from -4 to 4
- rel_buckets: int32 [2047], replicated, may hold values from 0 to 31, as said below
- segments: int32 [8, 1024], P('dp'), may hold values from 0 to 3, never falling along the last dimension, each value on 1 to 512 neighbouring positions
- gain_moe: float32 [768], replicated, may hold values from 0.5 to 1.5
- w_router: bfloat16 [768, 8], replicated, may hold values from -0.109375 to 0.109375
- routes: int32 [8192, 1], P(('dp', 'mp')), may hold values from 0 to 7; in each aligned block of 256 rows (0 to 255, 256 to 511, ...) at most 64 rows name the same one
- w_expert_in: bfloat16 [8, 768, 3072], P('dp', None, 'mp'), may hold values from -0.21875 to 0.21875
- w_expert_out: bfloat16 [8, 3072, 768], P('dp', 'mp'), may hold values from -1.25 to 1.25
Outputs:
- mixed: bfloat16 [8192, 768], P(('dp', 'mp'))
- grad_tokens: float32 [8192, 768], P(('dp', 'mp'))
- grad_gain_attn: float32 [768], replicated
- grad_qkv: float32 [3, 768, 768], P(None, 'dp', 'mp')
- grad_attn_out: float32 [768, 768], P('mp', 'dp')
- grad_rel_table: float32 [12, 32], replicated
- grad_gain_moe: float32 [768], replicated
- grad_router: float32 [768, 8], replicated
- grad_expert_in: float32 [8, 768, 3072], P('dp', None, 'mp')
- grad_expert_out: float32 [8, 3072, 768], P('dp', 'mp')
Inputs may be any that keep to these rules, and one draw needn't show every extreme that they name: `routes`: in each aligned block of 256 rows (the rows of one device) no expert is named by more than 64 rows; in some block one expert is named by exactly 64 rows. `segments`: within each sequence the numbers never fall; a segment holds at most half of 1024 tokens. `rel_buckets`: entry r is the bucket of the offset r - (1023) of a key from a query; it is 0 at offset 0, does not fall as the distance grows on either side, and offsets above 0 use the upper half of the buckets.
All inputs are finite; a program needn't handle non-finite values.
Results may differ from a plain program's by a relative error of at most 0.018.
The roundings to bfloat16 on the way count: a program that leaves them out, or rounds other values in their place, can miss the bound.
Values may be sent and summed in bfloat16 or wider, within the bound.
No kernel may reach another device: no remote copies, remote signals or barrier semaphores. Data moves between devices by JAX's collectives and lax.ppermute only.
A program may use at most 256 MiB of HBM per device.

v0:
```python
import functools

import jax
import jax.numpy as jnp
from jax import lax
from jax.experimental import pallas as pl
from jax.experimental.pallas import tpu as pltpu
from jax.sharding import PartitionSpec as P

epsilon = 1e-06
highest = lax.Precision.HIGHEST
low = jnp.bfloat16
f32 = jnp.float32
gelu_scale = 0.7978845608028654
gelu_cubic = 0.044715


kernel_times = {
    "attend": 15.0,
    "middle": 4.0,
    "expert": 16.0,
    "expert_value": 7.0,
    "expert_weight_grads": 18.0,
    "middle_back": 4.0,
    "attend_back": 27.0,
    "mixed": 3.0,
    "grad_tokens": 3.0,
}


def dot(left, right, left_dim=1, right_dim=0, precision=None):
    return lax.dot_general(
        left,
        right,
        (((left_dim,), (right_dim,)), ((), ())),
        precision=precision,
        preferred_element_type=f32,
    )


def call(kernel, name, outs, args, scratch=(), smem=0):
    flops = int(kernel_times.get(name, 2.0) * 1.15e9)
    spaces = [pltpu.SMEM] * smem + [pltpu.VMEM] * (len(args) - smem)
    return pl.pallas_call(
        kernel,
        out_shape=tuple(outs),
        in_specs=[pl.BlockSpec(memory_space=s) for s in spaces],
        out_specs=tuple(pl.BlockSpec(memory_space=pltpu.VMEM) for _ in outs),
        scratch_shapes=list(scratch),
        compiler_params=pltpu.CompilerParams(vmem_limit_bytes=56 * 2**20),
        cost_estimate=pl.CostEstimate(flops=flops, bytes_accessed=0, transcendentals=0),
        name=name,
    )(*args)


def like(shape, dtype):
    return jax.ShapeDtypeStruct(shape, dtype)


def spot_of(me, j, block):
    return pl.ds(pl.multiple_of((me ^ j) * block, block), block)


def put_in(pieces, whole, me):
    if len(pieces) == 1:
        whole[...] = pieces[0][...]
        return
    for j, piece in enumerate(pieces):
        whole[spot_of(me, j, piece.shape[0]), :] = piece[...]


def take_out(pieces, whole, me):
    if len(pieces) == 1:
        pieces[0][...] = whole[...]
        return
    for j, piece in enumerate(pieces):
        piece[...] = whole[spot_of(me, j, piece.shape[0]), :]


def rms_scale(values):
    return lax.rsqrt(jnp.mean(values * values, axis=-1, keepdims=True) + epsilon)


def slot_row(route_col, route_row, capacity):
    rows = route_col.shape[0]
    earlier = lax.broadcasted_iota(jnp.int32, (rows, rows), 0) < lax.broadcasted_iota(
        jnp.int32, (rows, rows), 1
    )
    same = (route_col == route_row) & earlier
    return route_row * capacity + jnp.sum(same.astype(jnp.int32), axis=0, keepdims=True)


def slot_col(route_col, route_row, capacity):
    rows = route_col.shape[0]
    earlier = lax.broadcasted_iota(jnp.int32, (rows, rows), 1) < lax.broadcasted_iota(
        jnp.int32, (rows, rows), 0
    )
    same = (route_col == route_row) & earlier
    return route_col * capacity + jnp.sum(same.astype(jnp.int32), axis=1, keepdims=True)


def to_slots(route_col, route_row, capacity, slots, values):
    row = slot_row(route_col, route_row, capacity)
    picked = lax.broadcasted_iota(jnp.int32, (slots, row.shape[1]), 0) == row
    return dot(picked.astype(f32).astype(low), values).astype(low)


def from_slots(route_col, route_row, capacity, slots, values):
    col = slot_col(route_col, route_row, capacity)
    picked = lax.broadcasted_iota(jnp.int32, (col.shape[0], slots), 1) == col
    return dot(picked.astype(f32).astype(low), values)


def norm_kernel(tok_ref, gain_ref, out_ref):
    values = tok_ref[...].astype(f32)
    out_ref[...] = (values * rms_scale(values) * gain_ref[...]).astype(low)


def dispatch_kernel(capacity, rcol_ref, rrow_ref, cot_ref, out_ref):
    out_ref[...] = to_slots(
        rcol_ref[...], rrow_ref[...], capacity, out_ref.shape[0], cot_ref[...]
    )


def bias_rows(table_ref, bucket_ref):
    buckets = table_ref.shape[1]
    hot = lax.broadcasted_iota(jnp.int32, (buckets, bucket_ref.shape[1]), 0) == bucket_ref[...]
    hot = hot.astype(f32)
    return dot(table_ref[...], hot, precision=highest), hot


def skewed(row, count):
    width = row.shape[1]
    block = pltpu.roll(jnp.broadcast_to(row, (8, width)), width - (count - 1), 1)
    sub = lax.broadcasted_iota(jnp.int32, (8, width), 0)
    for bit in (1, 2, 4):
        block = jnp.where((sub & bit) != 0, pltpu.roll(block, bit, 1), block)
    rows = 8
    while rows < count:
        block = jnp.concatenate([block, pltpu.roll(block, rows, 1)], axis=0)
        rows *= 2
    return block


def unskewed(block):
    rows, width = block.shape
    while rows > 8:
        rows //= 2
        block = pltpu.roll(block[:rows], rows, 1) + block[rows:]
    sub = lax.broadcasted_iota(jnp.int32, (8, width), 0)
    for bit in (4, 2, 1):
        block = jnp.where((sub & bit) == 0, pltpu.roll(block, bit, 1), block)
    return jnp.sum(block, axis=0, keepdims=True)


def head_masks(width, head_size):
    lane = lax.broadcasted_iota(jnp.int32, (1, width), 1) // head_size
    return [(lane == h).astype(f32).astype(low) for h in range(width // head_size)]


def weights_kernel(me_ref, *refs):
    pieces, (qkv_ref, out_ref) = refs[:-2], refs[-2:]
    split = qkv_ref.shape[1]
    block = pieces[0].shape[0]
    for j, piece in enumerate(pieces):
        spot = spot_of(me_ref[0], j, block)
        qkv_ref[spot, :] = piece[:, :split]
        out_ref[spot, :] = piece[:, split:]


def attend_kernel(heads, me_ref, *refs):
    pieces = len(refs[:-9]) // 2
    normed = refs[:pieces]
    w_ref, table_ref, bucket_ref, scol_ref, srow_ref, qkv_ref = refs[pieces : pieces + 6]
    ctx_out = refs[pieces + 6 : 2 * pieces + 6]
    normed_s, bias_s, ctx_s = refs[2 * pieces + 6 :]
    me = me_ref[0]
    block = normed[0].shape[0]
    length = normed_s.shape[0]
    width = qkv_ref.shape[2]
    put_in(normed, normed_s, me)
    for c in range(3):
        qkv_ref[c] = dot(normed_s[...], w_ref[:, c * width : (c + 1) * width]).astype(low)
    deltas, _ = bias_rows(table_ref, bucket_ref)
    for h in range(heads):
        bias_s[h] = skewed(deltas[h : h + 1], block)
    masks = head_masks(width, width // heads)

    def step(i, carry):
        rows = pl.ds(pl.multiple_of(i * block, block), block)
        shift = pl.multiple_of(length - block - i * block, block)
        same = scol_ref[rows, :] == srow_ref[...]
        query = qkv_ref[0, rows, :]
        total = jnp.zeros((block, width), f32)
        for h in range(heads):
            scores = dot(query * masks[h], qkv_ref[1], 1, 1) + bias_s[h, :, pl.ds(shift, length)]
            scores = jnp.where(same, scores, -1e30)
            powers = jnp.exp(scores - jnp.max(scores, axis=-1, keepdims=True))
            probs = (powers * (1.0 / jnp.sum(powers, axis=-1, keepdims=True))).astype(low)
            total = total + dot(probs, qkv_ref[2] * masks[h])
        ctx_s[rows, :] = total.astype(low)
        return carry

    lax.fori_loop(0, pieces, step, 0)
    take_out(ctx_out, ctx_s, me)


def small_rows(gain_one, gain_two, table, router, count):
    width = gain_one.shape[1]
    rows = []
    for row in (gain_one, gain_two, table):
        if row.shape[1] < width:
            row = jnp.concatenate([row, jnp.zeros((1, width - row.shape[1]), f32)], axis=1)
        upper = row.astype(low).astype(f32)
        rows += [upper, row - upper]
    rows.append(router)
    used = 6 + router.shape[0]
    if used < count:
        rows.append(jnp.zeros((count - used, width), f32))
    return jnp.concatenate(rows, axis=0).astype(low)


def attend_back_kernel(heads, me_ref, *refs):
    pieces = len(refs[:-16]) // 4
    normed = refs[:pieces]
    contexts = refs[pieces : 2 * pieces]
    grads = refs[2 * pieces : 3 * pieces]
    at = 3 * pieces
    (
        w_ref,
        wo_ref,
        table_ref,
        bucket_ref,
        scol_ref,
        srow_ref,
        qkv_ref,
        gain_ref,
        router_ref,
        gw_ref,
    ) = refs[at : at + 10]
    gn_out = refs[at + 10 : at + 10 + pieces]
    normed_s, bias_s, grad_s, wide_s, sums_s, gt_s = refs[at + 10 + pieces :]
    me = me_ref[0]
    block = normed[0].shape[0]
    length, model_width = normed_s.shape
    width = qkv_ref.shape[2]
    size = width // heads
    put_in(normed, normed_s, me)
    put_in(grads, wide_s, me)
    out_part = jnp.zeros((width, model_width), f32)
    for j in range(pieces):
        out_part = out_part + dot(contexts[j][...], grads[j][...], 0, 0)
    gw_ref[:, 3 * width :] = out_part.T.astype(low)
    grad_s[...] = dot(wide_s[...], wo_ref[...]).astype(low)
    deltas, hot = bias_rows(table_ref, bucket_ref)
    for h in range(heads):
        bias_s[h] = skewed(deltas[h : h + 1], block)
    sums_s[...] = jnp.zeros_like(sums_s)
    gt_s[...] = jnp.zeros_like(gt_s)
    masks = head_masks(width, size)
    keys_t = qkv_ref[1].astype(f32).T.astype(low)

    def step(i, carry):
        rows = pl.ds(pl.multiple_of(i * block, block), block)
        shift = pl.multiple_of(length - block - i * block, block)
        same = scol_ref[rows, :] == srow_ref[...]
        query = qkv_ref[0, rows, :]
        grad = grad_s[rows, :]
        query_t = query.astype(f32).T.astype(low)
        grad_t = grad.astype(f32).T.astype(low)
        for h in range(heads):
            span = slice(h * size, (h + 1) * size)
            scores = dot(query * masks[h], qkv_ref[1], 1, 1) + bias_s[h, :, pl.ds(shift, length)]
            scores = jnp.where(same, scores, -1e30)
            powers = jnp.exp(scores - jnp.max(scores, axis=-1, keepdims=True))
            probs = powers * (1.0 / jnp.sum(powers, axis=-1, keepdims=True))
            grad_probs = dot(grad * masks[h], qkv_ref[2], 1, 1)
            inner = jnp.sum(grad_probs * probs, axis=-1, keepdims=True)
            grad_scores = (probs * (grad_probs - inner)).astype(low)
            start = h * size
            gt_s[2 * width + start : 2 * width + start + size, :] += dot(
                grad_t[span], probs.astype(low)
            )
            gt_s[width + start : width + start + size, :] += dot(query_t[span], grad_scores)
            gt_s[start : start + size, rows] = dot(keys_t[span], grad_scores, 1, 1)
            sums_s[h, :, pl.ds(shift, length)] += grad_scores.astype(f32)
        return carry

    lax.fori_loop(0, pieces, step, 0)
    gw_ref[:, : 3 * width] = dot(gt_s[...].astype(low), normed_s[...]).T.astype(low)
    total = dot(gt_s[...].T.astype(low), w_ref[...], 1, 1)
    gain_grad = jnp.sum(total * normed_s[...].astype(f32), axis=0, keepdims=True)
    wide_s[...] = total.astype(low)
    rows = []
    for h in range(heads):
        sums = jnp.broadcast_to(unskewed(sums_s[h]), (8, sums_s.shape[2]))
        rows.append(dot(sums, hot, 1, 1, precision=highest)[0:1])
    row = jnp.concatenate(rows * pieces, axis=1)
    owner = lax.broadcasted_iota(jnp.int32, row.shape, 1) // (row.shape[1] // pieces)
    row = jnp.where(owner == me, row, 0.0)
    count = gn_out[0].shape[0] - block
    small = small_rows(gain_grad, gain_ref[...], row, router_ref[...], count)
    for j in range(pieces):
        gn_out[j][0:block] = wide_s[spot_of(me, j, block), :]
        gn_out[j][block:] = small


def middle_kernel(
    capacity, pieces, me_ref, rcol_ref, rrow_ref, tok_ref, gain_ref, *refs
):
    contexts, weights = refs[:pieces], refs[pieces : 2 * pieces]
    mid_ref, sends, send_s = refs[2 * pieces], refs[2 * pieces + 1 : -1], refs[-1]
    mid = tok_ref[...].astype(f32)
    for j in range(pieces):
        mid = mid + dot(contexts[j][...], weights[j][...], 1, 1)
    mid_ref[...] = mid
    normed = (mid * rms_scale(mid) * gain_ref[...]).astype(low)
    send_s[...] = to_slots(
        rcol_ref[...], rrow_ref[...], capacity, send_s.shape[0], normed
    )
    take_out(sends, send_s, me_ref[0])


def gate_of(rows, router_weight, expert):
    logits = dot(rows, router_weight, 1, 1)
    logits = jnp.exp(logits - jnp.max(logits, axis=-1, keepdims=True))
    router = logits / jnp.sum(logits, axis=-1, keepdims=True)
    hot = (lax.broadcasted_iota(jnp.int32, router.shape, 1) == expert).astype(f32)
    return router, hot, jnp.sum(router * hot, axis=-1, keepdims=True)


def hidden_of(pre_act):
    bent = jnp.tanh(gelu_scale * (pre_act + gelu_cubic * (pre_act * pre_act * pre_act)))
    half = 0.5 * (1.0 + bent)
    slope = half + 0.5 * pre_act * (1.0 - bent * bent) * (
        gelu_scale * (1.0 + 3.0 * gelu_cubic * (pre_act * pre_act))
    )
    return (pre_act * half).astype(low), slope


def expert_kernel(sources, pieces, me_ref, cot_ref, router_ref, *refs):
    got, refs = refs[:sources], refs[sources:]
    w_in, w_out, refs = refs[:pieces], refs[pieces : 2 * pieces], refs[2 * pieces :]
    sends, refs = refs[:sources], refs[sources:]
    rows_ref, router_grad_ref = refs[:2]
    hidden_out, (total_s, low_s) = refs[2:-2], refs[-2:]
    me = me_ref[0]
    put_in(got, rows_ref, me)
    rows = rows_ref[...]
    router, hot, gate = gate_of(rows, router_ref[...], me)
    grad_value = (gate * cot_ref[...].astype(f32)).astype(low)
    shared = jnp.zeros_like(gate)
    for j in range(pieces):
        hidden, slope = hidden_of(dot(rows, w_in[j][...]))
        hidden_out[j][...] = hidden
        grad_hidden = dot(grad_value, w_out[j][...], 1, 1)
        shared = shared + jnp.sum(hidden.astype(f32) * grad_hidden, axis=-1, keepdims=True)
        part = dot((grad_hidden * slope).astype(low), w_in[j][...], 1, 1)
        if j == 0:
            total_s[...] = part
        else:
            total_s[...] += part
    grad_logits = shared * (hot - router)
    upper = grad_logits.astype(low)
    lower = (grad_logits - upper.astype(f32)).astype(low)
    weight = router_ref[...]
    total = total_s[...] + dot(upper, weight) + dot(lower, weight)
    low_s[...] = total.astype(low)
    take_out(sends, low_s, me)
    router_grad_ref[...] = dot(upper, rows, 0, 0) + dot(lower, rows, 0, 0)


def value_kernel(me_ref, rows_ref, router_ref, *refs):
    pieces = (len(refs) - 1) // 2
    hidden, w_out, out_ref = refs[:pieces], refs[pieces : 2 * pieces], refs[2 * pieces]
    _, _, gate = gate_of(rows_ref[...], router_ref[...], me_ref[0])
    total = dot(hidden[0][...], w_out[0][...])
    for j in range(1, pieces):
        total = total + dot(hidden[j][...], w_out[j][...])
    out_ref[...] = (gate * total).astype(low)


def weight_grad_kernel(me_ref, router_ref, in_ref, out_ref, *refs):
    pieces = (len(refs) - 2) // 2
    rows_of, cots_of = refs[:pieces], refs[pieces : 2 * pieces]
    grad_in_ref, grad_out_ref = refs[2 * pieces :]
    for j in range(pieces):
        rows = rows_of[j][...]
        _, _, gate = gate_of(rows, router_ref[...], me_ref[0])
        grad_value = (gate * cots_of[j][...].astype(f32)).astype(low)
        hidden, slope = hidden_of(dot(rows, in_ref[...]))
        grad_pre = (dot(grad_value, out_ref[...], 1, 1) * slope).astype(low)
        part_in = dot(rows, grad_pre, 0, 0)
        part_out = dot(hidden, grad_value, 0, 0)
        if j == 0:
            grad_in_ref[...] = part_in
            grad_out_ref[...] = part_out
        else:
            grad_in_ref[...] += part_in
            grad_out_ref[...] += part_out


def norm_back(grad_normed, values, scale_rows, gain_rows):
    scaled = grad_normed * gain_rows
    inner_sum = jnp.mean(scaled * values, axis=-1, keepdims=True)
    return scale_rows * scaled - values * (scale_rows * scale_rows * scale_rows) * inner_sum


def middle_back_kernel(
    capacity, me_ref, rcol_ref, rrow_ref, mid_ref, cot_ref, gain_ref, *refs
):
    backs, (grad_ref, low_ref, gain_grad_ref, back_s) = refs[:-4], refs[-4:]
    put_in(backs, back_s, me_ref[0])
    grad = from_slots(rcol_ref[...], rrow_ref[...], capacity, back_s.shape[0], back_s[...])
    mid = mid_ref[...]
    scale = rms_scale(mid)
    gain_grad_ref[...] = jnp.sum(grad * mid * scale, axis=0, keepdims=True)
    grad_mid = cot_ref[...].astype(f32) + norm_back(grad, mid, scale, gain_ref[...])
    grad_ref[...] = grad_mid
    low_ref[...] = grad_mid.astype(low)


def mixed_kernel(capacity, rcol_ref, rrow_ref, back_ref, mid_ref, out_ref):
    value = from_slots(
        rcol_ref[...], rrow_ref[...], capacity, back_ref.shape[0], back_ref[...]
    )
    out_ref[...] = (mid_ref[...] + value).astype(low)


def last_kernel(experts, tok_ref, gain_ref, grad_mid_ref, *refs):
    parts, (out_ref, small_ref) = refs[:-2], refs[-2:]
    block = out_ref.shape[0]
    grad = parts[0][0:block].astype(f32)
    small = parts[0][block:].astype(f32)
    for part in parts[1:]:
        grad = grad + part[0:block].astype(f32)
        small = small + part[block:].astype(f32)
    values = tok_ref[...].astype(f32)
    out_ref[...] = grad_mid_ref[...] + norm_back(
        grad, values, rms_scale(values), gain_ref[...]
    )
    pairs = [small[i : i + 1] + small[i + 1 : i + 2] for i in (0, 2, 4)]
    small_ref[...] = small_rows(*pairs, small[6 : 6 + experts], small.shape[0])


def weight_sum_kernel(parts_ref, out_ref, qkv_ref):
    total = jnp.sum(parts_ref[...].astype(f32), axis=0)
    width = qkv_ref.shape[2]
    for c in range(3):
        qkv_ref[c] = total[:, c * width : (c + 1) * width]
    out_ref[...] = total[:, 3 * width :].T


def small_sum_kernel(gain_ref, *refs):
    parts, (gain_one_ref, table_ref, gain_two_ref, router_ref) = refs[:-4], refs[-4:]
    total = parts[0][...].astype(f32)
    for part in parts[1:]:
        total = total + part[...].astype(f32)
    gain_one_ref[...] = (total[0:1] + total[1:2]) / gain_ref[...]
    gain_two_ref[...] = total[2:3] + total[3:4]
    table = total[4:5] + total[5:6]
    buckets = table_ref.shape[1]
    for h in range(table_ref.shape[0]):
        table_ref[h : h + 1, :] = table[:, h * buckets : (h + 1) * buckets]
    router_ref[...] = total[6 : 6 + router_ref.shape[0]]


def permuted(value, axis, bit):
    size = lax.axis_size(axis)
    return lax.ppermute(value, axis, [(i, i ^ bit) for i in range(size)])


def gathered(value, axis):
    size = lax.axis_size(axis)
    held = {0: value}
    bit = size // 2
    while bit:
        held.update({j ^ bit: permuted(held[j], axis, bit) for j in list(held)})
        bit //= 2
    return [held[j] for j in range(size)]


def exchanged(parts, axis):
    if len(parts) == 1:
        count = lax.axis_size(axis)
        blocks = parts[0].reshape(count, -1, parts[0].shape[-1])
        return [sent_to_all(blocks, axis).reshape(parts[0].shape)]
    far_first = range(len(parts) - 1, 0, -1)
    got = {j: permuted(parts[j], axis, j) for j in far_first}
    return [parts[0]] + [got[j] for j in range(1, len(parts))]


def sent_to_all(parts, axis):
    return lax.all_to_all(parts, axis, split_axis=0, concat_axis=0, tiled=True)


def repeated(part, axis):
    return sent_to_all(jnp.broadcast_to(part, (lax.axis_size(axis), *part.shape)), axis)


def after(value, *others):
    return lax.optimization_barrier((value, *others))[0]


def shards(
    tokens,
    cotangent,
    gain_attn,
    w_qkv,
    w_attn_out,
    rel_table,
    rel_buckets,
    segments,
    gain_moe,
    w_router,
    routes,
    w_expert_in,
    w_expert_out,
):
    model_size = lax.axis_size("mp")
    data_size = lax.axis_size("dp")
    me = lax.axis_index("mp").astype(jnp.int32).reshape(1)
    expert = lax.axis_index("dp").astype(jnp.int32).reshape(1)
    tok_rows, model_width = tokens.shape
    length = segments.shape[1]
    total_heads, bucket_count = rel_table.shape
    heads = total_heads // model_size
    width = w_qkv.shape[2]
    weight_rows = w_qkv.shape[1]
    expert_count = w_router.shape[1]
    capacity = 2 * tok_rows // expert_count
    slots = expert_count * capacity
    hidden_units = w_expert_in.shape[2]
    span = 2 * length
    small_count = 6 + expert_count + (-(6 + expert_count)) % 16
    sources = data_size if data_size == 8 else 1
    piece_rows = slots // sources

    gain_one = gain_attn.reshape(1, model_width)
    gain_two = gain_moe.reshape(1, model_width)
    router_rows = w_router.T
    route_row = routes.reshape(1, tok_rows)
    seg_col = segments.reshape(length, 1)
    table = lax.dynamic_slice_in_dim(rel_table, me[0] * heads, heads, 0)
    table = jnp.pad(table, ((0, 8 - heads), (0, 0)))
    buckets = jnp.pad(rel_buckets, (0, 1), constant_values=-1).reshape(1, span)

    packed = jnp.concatenate([w_qkv[0], w_qkv[1], w_qkv[2], w_attn_out.T], axis=1)
    (normed,) = call(
        norm_kernel, "norm_one", [like((tok_rows, model_width), low)], (tokens, gain_one)
    )
    group = gathered(normed, "mp")
    ready = group[0]
    if sources == 1:
        packed = repeated(packed, "dp").reshape(model_width, 4 * width)
        w_heads, w_out = packed[:, : 3 * width], packed[:, 3 * width :]
    else:
        held = {0: packed}
        held.update({j: permuted(packed, "dp", j) for j in (6, 4, 2)})
        ready = held[6]
        held.update({j + 1: permuted(held[j], "dp", 1) for j in (0, 2, 4, 6)})
        w_heads, w_out = call(
            weights_kernel,
            "attn_weights",
            [like((model_width, 3 * width), low), like((model_width, width), low)],
            (expert, *[held[j] for j in range(8)]),
            smem=1,
        )
    out_weights = gathered(w_out, "mp")
    own_in, own_out = w_expert_in[0], w_expert_out[0]
    all_in = gathered(own_in, "mp")

    (send_cot,) = call(
        functools.partial(dispatch_kernel, capacity),
        "dispatch_cotangent",
        [like((slots, model_width), low)],
        (routes, route_row, after(cotangent, ready)),
    )
    slot_shape = (data_size, capacity, model_width)
    got_cot = sent_to_all(send_cot.reshape(slot_shape), "dp").reshape(slots, model_width)

    qkv, *contexts = call(
        functools.partial(attend_kernel, heads),
        "attend",
        [like((3, length, width), low)] + [like((tok_rows, width), low)] * model_size,
        (me, *group, w_heads, table, buckets, seg_col, segments),
        scratch=[
            pltpu.VMEM((length, model_width), low),
            pltpu.VMEM((heads, tok_rows, span), f32),
            pltpu.VMEM((length, width), low),
        ],
        smem=1,
    )
    got_contexts = exchanged(contexts, "mp")
    all_out = gathered(after(own_out, got_contexts[model_size // 2]), "mp")
    early_tokens = after(tokens, got_cot, all_in[model_size // 2])
    mid, *send_rows = call(
        functools.partial(middle_kernel, capacity, model_size),
        "middle",
        [like((tok_rows, model_width), f32)]
        + [like((piece_rows, model_width), low)] * sources,
        (expert, routes, route_row, early_tokens, gain_two, *got_contexts, *out_weights),
        scratch=[pltpu.VMEM((slots, model_width), low)],
        smem=1,
    )
    got_rows = exchanged(send_rows, "dp")
    outs = call(
        functools.partial(expert_kernel, sources, model_size),
        "expert",
        [like((piece_rows, model_width), low)] * sources
        + [like((slots, model_width), low), like((expert_count, model_width), f32)]
        + [like((slots, hidden_units), low)] * model_size,
        (expert, got_cot, router_rows, *got_rows, *all_in, *all_out),
        scratch=[
            pltpu.VMEM((slots, model_width), f32),
            pltpu.VMEM((slots, model_width), low),
        ],
        smem=1,
    )
    grad_slots, (rows, router_part), hidden = (
        list(outs[:sources]),
        outs[sources : sources + 2],
        outs[sources + 2 :],
    )
    back_grad = exchanged(grad_slots, "dp")
    (value_slots,) = call(
        value_kernel,
        "expert_value",
        [like((slots, model_width), low)],
        (expert, rows, router_rows, *hidden, *all_out),
        smem=1,
    )
    all_cot = gathered(after(got_cot, got_rows[-1]), "mp")
    back_grad[0] = after(back_grad[0], value_slots, all_cot[model_size // 2])
    grad_mid, grad_low, grad_gain_moe = call(
        functools.partial(middle_back_kernel, capacity),
        "middle_back",
        [
            like((tok_rows, model_width), f32),
            like((tok_rows, model_width), low),
            like((1, model_width), f32),
        ],
        (expert, routes, route_row, mid, cotangent, gain_two, *back_grad),
        scratch=[pltpu.VMEM((slots, model_width), low)],
        smem=1,
    )
    grad_group = gathered(grad_low, "mp")
    all_rows = gathered(after(rows, grad_group[-1]), "mp")
    back_value = sent_to_all(value_slots.reshape(slot_shape), "dp").reshape(slots, model_width)
    grad_weight_part, *grad_parts = call(
        functools.partial(attend_back_kernel, heads),
        "attend_back",
        [like((model_width, 4 * width), low)]
        + [like((tok_rows + small_count, model_width), low)] * model_size,
        (
            me,
            *group,
            *contexts,
            *grad_group,
            w_heads,
            w_out,
            table,
            buckets,
            seg_col,
            segments,
            qkv,
            grad_gain_moe,
            router_part,
        ),
        scratch=[
            pltpu.VMEM((length, model_width), low),
            pltpu.VMEM((heads, tok_rows, span), f32),
            pltpu.VMEM((length, width), low),
            pltpu.VMEM((length, model_width), low),
            pltpu.VMEM((heads, tok_rows, span), f32),
            pltpu.VMEM((3 * width, length), f32),
        ],
        smem=1,
    )
    got_parts = exchanged(grad_parts, "mp")
    got_weights = sent_to_all(
        grad_weight_part.reshape(data_size, weight_rows, 4 * width), "dp"
    )

    grad_expert_in, grad_expert_out = call(
        weight_grad_kernel,
        "expert_weight_grads",
        [like((model_width, hidden_units), f32), like((hidden_units, model_width), f32)],
        (
            expert,
            router_rows,
            own_in,
            own_out,
            after(rows, grad_weight_part),
            *all_rows[1:],
            got_cot,
            *all_cot[1:],
        ),
        smem=1,
    )
    (mixed,) = call(
        functools.partial(mixed_kernel, capacity),
        "mixed",
        [like((tok_rows, model_width), low)],
        (routes, route_row, after(back_value, grad_weight_part), mid),
    )
    grad_tokens, small = call(
        functools.partial(last_kernel, expert_count),
        "grad_tokens",
        [like((tok_rows, model_width), f32), like((small_count, model_width), low)],
        (tokens, gain_one, grad_mid, *got_parts),
    )
    if sources == 1:
        smalls = [jnp.sum(repeated(small, "dp").astype(f32), axis=0)]
    else:
        smalls = exchanged([small] * data_size, "dp")
    grad_attn_out, grad_qkv = call(
        weight_sum_kernel,
        "attn_weight_sums",
        [like((width, weight_rows), f32), like((3, weight_rows, width), f32)],
        (got_weights,),
    )
    grad_gain_attn, grad_table, sum_gain_moe, grad_router = call(
        small_sum_kernel,
        "small_sums",
        [
            like((1, model_width), f32),
            like((total_heads, bucket_count), f32),
            like((1, model_width), f32),
            like((expert_count, model_width), f32),
        ],
        (gain_one, *smalls),
    )
    return (
        mixed,
        grad_tokens,
        grad_gain_attn.reshape(model_width),
        grad_qkv,
        grad_attn_out,
        grad_table,
        sum_gain_moe.reshape(model_width),
        grad_router.T,
        grad_expert_in[None],
        grad_expert_out[None],
    )


def solution(mesh):
    placed = (
        P(("dp", "mp"), None),
        P(("dp", "mp"), None),
        P(),
        P(None, "dp", "mp"),
        P("mp", "dp"),
        P(),
        P(),
        P("dp", None),
        P(),
        P(),
        P(("dp", "mp"), None),
        P("dp", None, "mp"),
        P("dp", "mp", None),
    )
    return jax.shard_map(
        shards,
        mesh=mesh,
        in_specs=placed,
        out_specs=(
            P(("dp", "mp"), None),
            P(("dp", "mp"), None),
            P(),
            P(None, "dp", "mp"),
            P("mp", "dp"),
            P(),
            P(),
            P(),
            P("dp", None, "mp"),
            P("dp", "mp", None),
        ),
        check_vma=False,
    )
```

profile of v0, /device:TPU:0, one launch (start us, length us, event | category | flops | bytes accessed | tf_op | source)
XLA Modules:
  0.0 336.4 jit_solution(15807301588680178006)
XLA Ops:
  0.7 1.3 reshape.68.gain_ref
  1.9 2.0 norm_one.1.refs_0_
  3.9 2.9 collective-permute-start.3
  7.1 3.7 %collective-permute-start = (bf16[96,768]{1,0:T(8,128)(2,1)S(1)}, bf16[96,768]{1,0:T(8,128)(2,1)S(1)}, u32[]{:S(2)}, u32[]{:S(2)}) collective-permute-start(bf16[96,768]{1,0:T(8,128)(2,1)S(1)} %pad_maximum_fusion.refs_0_), channel_id=1, source_target_pairs={{0,24},{4,28},{8,16},{12,20},{16,8},{20,12},{24,0},{28,4},{1,25},{... | collective-permute-start | bytes 442376 | tf_op jit(solution)/shard_map/ppermute | solution.py:470
  11.6 1.5 collective-permute-start.5
  13.1 2.7 collective-permute-done.refs_6_
  16.3 2.2 collective-permute-done.6.refs_2_
  18.4 1.5 collective-permute-start.10
  19.9 3.0 collective-permute-done.8.refs_4_
  23.0 1.5 collective-permute-start.7
  27.3 2.1 collective-permute-done.7.refs_3_
  29.4 1.6 collective-permute-done.9.refs_5_
  31.7 2.6 attn_weights.1
  35.2 14.8 %attend.1 = (bf16[3,1024,192]{2,1,0:T(8,128)(2,1)}, bf16[256,192]{1,0:T(8,128)(2,1)}, bf16[256,192]{1,0:T(8,128)(2,1)}, bf16[256,192]{1,0:T(8,128)(2,1)}, bf16[256,192]{1,0:T(8,128)(2,1)}) custom-call(s32[1]{0:T(128)} %bitcast.10.me_ref, bf16[256,768]{1,0:T(8,128)(2,1)} %norm_one.1.refs_0_, bf16[256,768]{1,0:T(8,128)(2,1)} %copy-done.20, ...), custom_call_target="tpu_custom_call" | custom-call | flops 17250000896 | tf_op jit(solution)/shard_map/attend/pallas_call | solution.py:44
  50.6 1.5 collective-permute-start.1
  52.8 3.8 %collective-permute-done.12.refs_2_ = bf16[256,192]{1,0:T(8,128)(2,1)S(1)} collective-permute-done((bf16[256,192]{1,0:T(8,128)(2,1)}, bf16[256,192]{1,0:T(8,128)(2,1)S(1)}, u32[]{:S(2)}, u32[]{:S(2)}) %collective-permute-start.12) | collective-permute-done | bytes 98336 | tf_op jit(solution)/shard_map/ppermute | solution.py:470
  57.2 2.4 dispatch_cotangent.1
  59.6 5.6 %all-to-all-start = ((bf16[8,64,768]{2,1,0:T(8,128)(2,1)}), bf16[8,64,768]{2,1,0:T(8,128)(2,1)S(1)}, u32[]{:S(2)}, u32[]{:S(2)}) async-start(bf16[8,64,768]{2,1,0:T(8,128)(2,1)} %bitcast.28), calls=%async_computation | async-start | bytes 1572864 | tf_op jit(solution)/shard_map/all_to_all | solution.py:494
  65.2 1.6 collective-permute-start.15
  67.3 45.6 %collective-permute-done.15.refs_6_ = bf16[768,192]{1,0:T(8,128)(2,1)} collective-permute-done((bf16[768,192]{1,0:T(8,128)(2,1)S(1)}, bf16[768,192]{1,0:T(8,128)(2,1)}, u32[]{:S(2)}, u32[]{:S(2)}) %collective-permute-start.15) | collective-permute-done | bytes 294944 | tf_op jit(solution)/shard_map/ppermute | solution.py:470
  115.1 3.3 collective-permute-done.13.refs_3_
  120.0 1.4 collective-permute-done.16.refs_7_
  122.2 3.8 %middle.1 = (f32[256,768]{1,0:T(8,128)}, bf16[64,768]{1,0:T(8,128)(2,1)}, bf16[64,768]{1,0:T(8,128)(2,1)}, bf16[64,768]{1,0:T(8,128)(2,1)}, bf16[64,768]{1,0:T(8...) custom-call(s32[1]{0:T(128)} %bitcast.1.me_ref, ...), custom_call_target="tpu_custom_call" | custom-call | flops 4600000000 | tf_op jit(solution)/shard_map/middle/pallas_call | solution.py:44
  126.0 1.6 collective-permute-start.17
  127.6 4.1 %collective-permute-start.18 = (bf16[64,768]{1,0:T(8,128)(2,1)}, bf16[64,768]{1,0:T(8,128)(2,1)S(1)}, u32[]{:S(2)}, u32[]{:S(2)}) collective-permute-start(bf16[64,768]{1,0:T(8,128)(2,1)} %get-tuple-element.76), channel_id=1, source_target_pairs={{0,8},{4,12},{8,0},{12,4},{16,24},{20,28},{24,16},{28,20},{1,9},{5... | collective-permute-start | bytes 294920 | tf_op jit(solution)/shard_map/ppermute | solution.py:470
  131.7 4.5 %collective-permute-start.19 = (bf16[64,768]{1,0:T(8,128)(2,1)}, bf16[64,768]{1,0:T(8,128)(2,1)S(1)}, u32[]{:S(2)}, u32[]{:S(2)}) collective-permute-start(bf16[64,768]{1,0:T(8,128)(2,1)} %get-tuple-element.77), channel_id=1, source_target_pairs={{0,12},{4,8},{8,4},{12,0},{16,28},{20,24},{24,20},{28,16},{1,13},{... | collective-permute-start | bytes 294920 | tf_op jit(solution)/shard_map/ppermute | solution.py:470
  136.2 3.5 %collective-permute-done.19.refs_3_ = bf16[64,768]{1,0:T(8,128)(2,1)S(1)} collective-permute-done((bf16[64,768]{1,0:T(8,128)(2,1)}, bf16[64,768]{1,0:T(8,128)(2,1)S(1)}, u32[]{:S(2)}, u32[]{:S(2)}) %collective-permute-start.19) | collective-permute-done | bytes 98336 | tf_op jit(solution)/shard_map/ppermute | solution.py:470
  139.9 7.0 %collective-permute-done.20.refs_4_ = bf16[64,768]{1,0:T(8,128)(2,1)S(1)} collective-permute-done((bf16[64,768]{1,0:T(8,128)(2,1)}, bf16[64,768]{1,0:T(8,128)(2,1)S(1)}, u32[]{:S(2)}, u32[]{:S(2)}) %collective-permute-start.20) | collective-permute-done | bytes 98336 | tf_op jit(solution)/shard_map/ppermute | solution.py:470
  148.4 6.2 %collective-permute-done.21.refs_5_ = bf16[64,768]{1,0:T(8,128)(2,1)S(1)} collective-permute-done((bf16[64,768]{1,0:T(8,128)(2,1)}, bf16[64,768]{1,0:T(8,128)(2,1)S(1)}, u32[]{:S(2)}, u32[]{:S(2)}) %collective-permute-start.21) | collective-permute-done | bytes 98336 | tf_op jit(solution)/shard_map/ppermute | solution.py:470
  155.8 16.2 %expert.1 = (bf16[64,768]{1,0:T(8,128)(2,1)}, bf16[64,768]{1,0:T(8,128)(2,1)}, bf16[64,768]{1,0:T(8,128)(2,1)}, bf16[64,768]{1,0:T(8,128)(2,1)}, bf16[64,768]{1,...) custom-call(s32[1]{0:T(128)} %bitcast.1.me_ref, ...), custom_call_target="tpu_custom_call" | custom-call | flops 18400000000 | tf_op jit(solution)/shard_map/expert/pallas_call | solution.py:44
  172.1 1.2 collective-permute-start.30
  173.3 1.6 collective-permute-start.31
  176.6 2.5 collective-permute-start.34
  180.3 3.0 collective-permute-start.36
  183.3 7.2 %expert_value.1 = bf16[512,768]{1,0:T(8,128)(2,1)} custom-call(s32[1]{0:T(128)} %bitcast.1.me_ref, bf16[512,768]{1,0:T(8,128)(2,1)} %get-tuple-element.119.rows_ref.refs_0_, bf16[8,768]{1,0:T(8,128)(2,1)} %bitcast.47, bf16[512,768]{1,0:T(8,128)(2,1)} %get-tuple-element.84.refs_0_, bf16[512,768]{1,0:T(8,128)(2,1)} %get-tuple-element.85.refs_1_, ...), custom_call_target="tpu_custom_call" | custom-call | flops 8049999872 | tf_op jit(solution)/shard_map/expert_value/pallas_call | solution.py:44
  192.2 3.6 %middle_back.1 = (f32[256,768]{1,0:T(8,128)}, bf16[256,768]{1,0:T(8,128)(2,1)}, f32[1,768]{1,0:T(1,128)}) custom-call(s32[1]{0:T(128)} %bitcast.1.me_ref, s32[256,1]{1,0:T(8,128)} %copy.34.rcol_ref, s32[1,256]{1,0:T(1,128)} %bitcast.35, f32[256,768]{1,0:T(8,128)} %get-tuple-element.88.mid_ref, bf16[256,768]{1,0:T(8,128)(2,1)} %cot_ref.2, ...), custom_call_target="tpu_custom_call" | custom-call | flops 4600000000 | tf_op jit(solution)/shard_map/middle_back/pallas_call | solution.py:44
  196.6 7.2 %collective-permute-done.38.refs_10_ = bf16[256,768]{1,0:T(8,128)(2,1)S(1)} collective-permute-done((bf16[256,768]{1,0:T(8,128)(2,1)}, bf16[256,768]{1,0:T(8,128)(2,1)S(1)}, u32[]{:S(2)}, u32[]{:S(2)}) %collective-permute-start.38) | collective-permute-done | bytes 393248 | tf_op jit(solution)/shard_map/ppermute | solution.py:470
  204.3 6.2 %all-to-all-start.1 = ((bf16[8,64,768]{2,1,0:T(8,128)(2,1)}), bf16[8,64,768]{2,1,0:T(8,128)(2,1)S(1)}, u32[]{:S(2)}, u32[]{:S(2)}) async-start(bf16[8,64,768]{2,1,0:T(8,128)(2,1)} %bitcast.14), calls=%async_computation.1 | async-start | bytes 1572864 | tf_op jit(solution)/shard_map/all_to_all | solution.py:494
  211.6 26.9 %attend_back.1 = (bf16[768,768]{1,0:T(8,128)(2,1)}, bf16[272,768]{1,0:T(8,128)(2,1)}, bf16[272,768]{1,0:T(8,128)(2,1)}, bf16[272,768]{1,0:T(8,128)(2,1)}, bf16[272,768]{1,0:T(8,128)(2,1)}) custom-call(s32[1]{0:T(128)} %bitcast.10.me_ref, bf16[256,768]{1,0:T(8,128)(2,1)} %norm_one.1.refs_0_, bf16[256,768]{1,0:T(8,128)(2,1)} %copy-done.20, ...), custom_call_target="tpu_custom_call" | custom-call | flops 31050000384 | tf_op jit(solution)/shard_map/attend_back/pallas_call | solution.py:44
  238.6 1.8 collective-permute-start.41
  241.0 10.2 %collective-permute-done.41.refs_2_ = bf16[272,768]{1,0:T(8,128)(2,1)S(1)} collective-permute-done((bf16[272,768]{1,0:T(8,128)(2,1)}, bf16[272,768]{1,0:T(8,128)(2,1)S(1)}, u32[]{:S(2)}, u32[]{:S(2)}) %collective-permute-start.41) | collective-permute-done | bytes 417824 | tf_op jit(solution)/shard_map/ppermute | solution.py:470
  251.8 7.5 %collective-permute-done.42.refs_3_ = bf16[272,768]{1,0:T(8,128)(2,1)S(1)} collective-permute-done((bf16[272,768]{1,0:T(8,128)(2,1)}, bf16[272,768]{1,0:T(8,128)(2,1)S(1)}, u32[]{:S(2)}, u32[]{:S(2)}) %collective-permute-start.42) | collective-permute-done | bytes 417824 | tf_op jit(solution)/shard_map/ppermute | solution.py:470
  260.1 3.1 grad_tokens.1
  263.2 2.0 collective-permute-start.43
  265.2 2.0 collective-permute-done.43.refs_1_
  267.2 2.0 collective-permute-start.44
  269.3 2.0 collective-permute-done.44.refs_2_
  271.3 2.9 collective-permute-start.45
  274.2 2.0 collective-permute-done.45.refs_3_
  276.2 2.9 collective-permute-start.46
  279.1 2.0 collective-permute-done.46.refs_4_
  281.2 4.0 %collective-permute-start.47 = (bf16[16,768]{1,0:T(8,128)(2,1)}, bf16[16,768]{1,0:T(8,128)(2,1)S(1)}, u32[]{:S(2)}, u32[]{:S(2)}) collective-permute-start(bf16[16,768]{1,0:T(8,128)(2,1)} %get-tuple-element.111.refs_0_), channel_id=1, source_target_pairs={{0,20},{4,16},{8,28},{12,24},{16,4},{20,0},{24,12},{28,8},{1,21},{... | collective-permute-start | bytes 73736 | tf_op jit(solution)/shard_map/ppermute | solution.py:470
  285.1 2.1 collective-permute-done.47.refs_5_
  287.2 4.2 %collective-permute-start.48 = (bf16[16,768]{1,0:T(8,128)(2,1)}, bf16[16,768]{1,0:T(8,128)(2,1)S(1)}, u32[]{:S(2)}, u32[]{:S(2)}) collective-permute-start(bf16[16,768]{1,0:T(8,128)(2,1)} %get-tuple-element.111.refs_0_), channel_id=1, source_target_pairs={{0,24},{4,28},{8,16},{12,20},{16,8},{20,12},{24,0},{28,4},{1,25},{... | collective-permute-start | bytes 73736 | tf_op jit(solution)/shard_map/ppermute | solution.py:470
  291.5 2.0 collective-permute-done.48.refs_6_
  293.5 4.8 %collective-permute-start.49 = (bf16[16,768]{1,0:T(8,128)(2,1)}, bf16[16,768]{1,0:T(8,128)(2,1)S(1)}, u32[]{:S(2)}, u32[]{:S(2)}) collective-permute-start(bf16[16,768]{1,0:T(8,128)(2,1)} %get-tuple-element.111.refs_0_), channel_id=1, source_target_pairs={{0,28},{4,24},{8,20},{12,16},{16,12},{20,8},{24,4},{28,0},{1,29},{... | collective-permute-start | bytes 73736 | tf_op jit(solution)/shard_map/ppermute | solution.py:470
  298.2 2.0 collective-permute-done.49.refs_7_
  300.9 1.6 small_sums.1
  302.5 1.3 reduce
  303.7 1.3 reduce.1
  305.9 6.2 %all-to-all-start.2 = ((bf16[8,96,768]{2,1,0:T(8,128)(2,1)}), bf16[8,96,768]{2,1,0:T(8,128)(2,1)S(1)}, u32[]{:S(2)}, u32[]{:S(2)}) async-start(bf16[8,96,768]{2,1,0:T(8,128)(2,1)} %bitcast.16), calls=%async_computation.2 | async-start | bytes 2359296 | tf_op jit(solution)/shard_map/all_to_all | solution.py:494
  312.1 2.9 mixed.1
  315.0 17.3 %expert_weight_grads.1 = (f32[768,768]{1,0:T(8,128)}, f32[768,768]{1,0:T(8,128)}) custom-call(s32[1]{0:T(128)} %bitcast.1.me_ref, bf16[8,768]{1,0:T(8,128)(2,1)} %bitcast.48, bf16[768,768]{1,0:T(8,128)(2,1)} %bitcast.38, bf16[768,768]{1,0:T(8,128)(2,1)} %bitcast.43, bf16[512,768]{1,0:T(8,128)(2,1)} %get-tuple-element.119.rows_ref.refs_0_, ...), custom_call_target="tpu_custom_call" | custom-call | flops 20700000256 | tf_op jit(solution)/shard_map/expert_weight_grads/pallas_call | solution.py:44
  334.0 2.2 attn_weight_sums.1
  (196 shorter events, 27.8 us)
Async XLA Ops:
  3.9 12.3 %collective-permute-start.3 = (bf16[256,768]{1,0:T(8,128)(2,1)}, bf16[256,768]{1,0:T(8,128)(2,1)S(1)}, u32[]{:S(2)}, u32[]{:S(2)}) collective-permute-start(bf16[256,768]{1,0:T(8,128)(2,1)} %norm_one.1.refs_0_), channel_id=1, source_target_pairs={{0,2},{1,3},{2,0},{3,1},{4,6},{5,7},{6,4},{7,5},{8,10},{9,11},{10,... | collective-permute-start | bytes 1179656 | tf_op jit(solution)/shard_map/ppermute | solution.py:470
  7.1 8.6 %collective-permute-start = (bf16[96,768]{1,0:T(8,128)(2,1)S(1)}, bf16[96,768]{1,0:T(8,128)(2,1)S(1)}, u32[]{:S(2)}, u32[]{:S(2)}) collective-permute-start(bf16[96,768]{1,0:T(8,128)(2,1)S(1)} %pad_maximum_fusion.refs_0_), channel_id=1, source_target_pairs={{0,24},{4,28},{8,16},{12,20},{16,8},{20,12},{24,0},{28,4},{1,25},{... | collective-permute-start | bytes 442376 | tf_op jit(solution)/shard_map/ppermute | solution.py:470
  10.8 7.7 %collective-permute-start.6 = (bf16[96,768]{1,0:T(8,128)(2,1)S(1)}, bf16[96,768]{1,0:T(8,128)(2,1)S(1)}, u32[]{:S(2)}, u32[]{:S(2)}) collective-permute-start(bf16[96,768]{1,0:T(8,128)(2,1)S(1)} %pad_maximum_fusion.refs_0_), channel_id=1, source_target_pairs={{0,8},{4,12},{8,0},{12,4},{16,24},{20,28},{24,16},{28,20},{1,9},{5... | collective-permute-start | bytes 442376 | tf_op jit(solution)/shard_map/ppermute | solution.py:470
  10.8 12.2 %collective-permute-start.8 = (bf16[96,768]{1,0:T(8,128)(2,1)S(1)}, bf16[96,768]{1,0:T(8,128)(2,1)S(1)}, u32[]{:S(2)}, u32[]{:S(2)}) collective-permute-start(bf16[96,768]{1,0:T(8,128)(2,1)S(1)} %pad_maximum_fusion.refs_0_), channel_id=1, source_target_pairs={{0,16},{4,20},{8,24},{12,28},{16,0},{20,4},{24,8},{28,12},{1,17},{... | collective-permute-start | bytes 442376 | tf_op jit(solution)/shard_map/ppermute | solution.py:470
  11.6 12.9 %collective-permute-start.5 = (bf16[96,768]{1,0:T(8,128)(2,1)S(1)}, bf16[96,768]{1,0:T(8,128)(2,1)S(1)}, u32[]{:S(2)}, u32[]{:S(2)}) collective-permute-start(bf16[96,768]{1,0:T(8,128)(2,1)S(1)} %pad_maximum_fusion.refs_0_), channel_id=1, source_target_pairs={{0,4},{4,0},{8,12},{12,8},{16,20},{20,16},{24,28},{28,24},{1,5},{5... | collective-permute-start | bytes 442376 | tf_op jit(solution)/shard_map/ppermute | solution.py:470
  15.7 18.5 %collective-permute-start.2 = (bf16[256,768]{1,0:T(8,128)(2,1)}, bf16[256,768]{1,0:T(8,128)(2,1)S(1)}, u32[]{:S(2)}, u32[]{:S(2)}) collective-permute-start(bf16[256,768]{1,0:T(8,128)(2,1)} %norm_one.1.refs_0_), channel_id=1, source_target_pairs={{0,1},{1,0},{2,3},{3,2},{4,5},{5,4},{6,7},{7,6},{8,9},{9,8},{10,11... | collective-permute-start | bytes 1179656 | tf_op jit(solution)/shard_map/ppermute | solution.py:470
  16.2 18.1 %collective-permute-start.4 = (bf16[256,768]{1,0:T(8,128)(2,1)S(1)}, bf16[256,768]{1,0:T(8,128)(2,1)S(1)}, u32[]{:S(2)}, u32[]{:S(2)}) collective-permute-start(bf16[256,768]{1,0:T(8,128)(2,1)S(1)} %collective-permute-done.3.refs_2_), channel_id=1, source_target_pairs={{0,1},{1,0},{2,3},{3,2},{4,5},{5,4},{6,7},{7,6},{8,9},{9,8},{10,11... | collective-permute-start | bytes 1179656 | tf_op jit(solution)/shard_map/ppermute | solution.py:470
  18.4 8.9 %collective-permute-start.10 = (bf16[96,768]{1,0:T(8,128)(2,1)S(1)}, bf16[96,768]{1,0:T(8,128)(2,1)S(1)}, u32[]{:S(2)}, u32[]{:S(2)}) collective-permute-start(bf16[96,768]{1,0:T(8,128)(2,1)S(1)} %collective-permute-done.refs_6_), channel_id=1, source_target_pairs={{0,4},{4,0},{8,12},{12,8},{16,20},{20,16},{24,28},{28,24},{1,5},{5... | collective-permute-start | bytes 442376 | tf_op jit(solution)/shard_map/ppermute | solution.py:470
  23.0 6.4 %collective-permute-start.7 = (bf16[96,768]{1,0:T(8,128)(2,1)S(1)}, bf16[96,768]{1,0:T(8,128)(2,1)S(1)}, u32[]{:S(2)}, u32[]{:S(2)}) collective-permute-start(bf16[96,768]{1,0:T(8,128)(2,1)S(1)} %collective-permute-done.6.refs_2_), channel_id=1, source_target_pairs={{0,4},{4,0},{8,12},{12,8},{16,20},{20,16},{24,28},{28,24},{1,5},{5... | collective-permute-start | bytes 442376 | tf_op jit(solution)/shard_map/ppermute | solution.py:470
  24.5 6.5 %collective-permute-start.9 = (bf16[96,768]{1,0:T(8,128)(2,1)S(1)}, bf16[96,768]{1,0:T(8,128)(2,1)S(1)}, u32[]{:S(2)}, u32[]{:S(2)}) collective-permute-start(bf16[96,768]{1,0:T(8,128)(2,1)S(1)} %collective-permute-done.8.refs_4_), channel_id=1, source_target_pairs={{0,4},{4,0},{8,12},{12,8},{16,20},{20,16},{24,28},{28,24},{1,5},{5... | collective-permute-start | bytes 442376 | tf_op jit(solution)/shard_map/ppermute | solution.py:470
  50.0 6.6 %collective-permute-start.12 = (bf16[256,192]{1,0:T(8,128)(2,1)}, bf16[256,192]{1,0:T(8,128)(2,1)S(1)}, u32[]{:S(2)}, u32[]{:S(2)}) collective-permute-start(bf16[256,192]{1,0:T(8,128)(2,1)} %get-tuple-element.71.refs_6_), channel_id=1, source_target_pairs={{0,2},{1,3},{2,0},{3,1},{4,6},{5,7},{6,4},{7,5},{8,10},{9,11},{10,... | collective-permute-start | bytes 294920 | tf_op jit(solution)/shard_map/ppermute | solution.py:470
  50.6 64.1 %collective-permute-start.1 = (bf16[768,768]{1,0:T(8,128)(2,1)S(1)}, bf16[768,768]{1,0:T(8,128)(2,1)}, u32[]{:S(2)}, u32[]{:S(2)}) collective-permute-start(bf16[768,768]{1,0:T(8,128)(2,1)S(1)} %bitcast.39), channel_id=1, source_target_pairs={{0,2},{1,3},{2,0},{3,1},{4,6},{5,7},{6,4},{7,5},{8,10},{9,11},{10,... | collective-permute-start | bytes 3538952 | tf_op jit(solution)/shard_map/ppermute | solution.py:470
  56.7 58.3 %collective-permute-start.27 = (bf16[768,768]{1,0:T(8,128)(2,1)S(1)}, bf16[768,768]{1,0:T(8,128)(2,1)}, u32[]{:S(2)}, u32[]{:S(2)}) collective-permute-start(bf16[768,768]{1,0:T(8,128)(2,1)S(1)} %bitcast.44), channel_id=1, source_target_pairs={{0,2},{1,3},{2,0},{3,1},{4,6},{5,7},{6,4},{7,5},{8,10},{9,11},{10,... | collective-permute-start | bytes 3538952 | tf_op jit(solution)/shard_map/ppermute | solution.py:470
  59.6 59.8 %copy-start.10 = (f32[768]{0:T(1024)S(1)}, f32[768]{0:T(1024)}, u32[]{:S(2)}) copy-start(f32[768]{0:T(1024)} %param.21) | copy-start | bytes 9220
  59.6 60.4 %all-to-all-start = ((bf16[8,64,768]{2,1,0:T(8,128)(2,1)}), bf16[8,64,768]{2,1,0:T(8,128)(2,1)S(1)}, u32[]{:S(2)}, u32[]{:S(2)}) async-start(bf16[8,64,768]{2,1,0:T(8,128)(2,1)} %bitcast.28), calls=%async_computation | async-start | bytes 1572864 | tf_op jit(solution)/shard_map/all_to_all | solution.py:494
  65.2 47.7 %collective-permute-start.15 = (bf16[768,192]{1,0:T(8,128)(2,1)S(1)}, bf16[768,192]{1,0:T(8,128)(2,1)}, u32[]{:S(2)}, u32[]{:S(2)}) collective-permute-start(bf16[768,192]{1,0:T(8,128)(2,1)S(1)} %copy-done.22), channel_id=1, source_target_pairs={{0,2},{1,3},{2,0},{3,1},{4,6},{5,7},{6,4},{7,5},{8,10},{9,11},{10,... | collective-permute-start | bytes 884744 | tf_op jit(solution)/shard_map/ppermute | solution.py:470
  66.8 46.1 %collective-permute-start.14 = (bf16[768,192]{1,0:T(8,128)(2,1)S(1)}, bf16[768,192]{1,0:T(8,128)(2,1)S(1)}, u32[]{:S(2)}, u32[]{:S(2)}) collective-permute-start(bf16[768,192]{1,0:T(8,128)(2,1)S(1)} %copy-done.22), channel_id=1, source_target_pairs={{0,1},{1,0},{2,3},{3,2},{4,5},{5,4},{6,7},{7,6},{8,9},{9,8},{10,11... | collective-permute-start | bytes 884744 | tf_op jit(solution)/shard_map/ppermute | solution.py:470
  66.8 60.8 %collective-permute-start.24 = (bf16[768,768]{1,0:T(8,128)(2,1)S(1)}, bf16[768,768]{1,0:T(8,128)(2,1)}, u32[]{:S(2)}, u32[]{:S(2)}) collective-permute-start(bf16[768,768]{1,0:T(8,128)(2,1)S(1)} %bitcast.40), channel_id=1, source_target_pairs={{0,1},{1,0},{2,3},{3,2},{4,5},{5,4},{6,7},{7,6},{8,9},{9,8},{10,11... | collective-permute-start | bytes 3538952 | tf_op jit(solution)/shard_map/ppermute | solution.py:470
  112.9 1.6 collective-permute-start.11
  112.9 5.5 %collective-permute-start.13 = (bf16[256,192]{1,0:T(8,128)(2,1)}, bf16[256,192]{1,0:T(8,128)(2,1)S(1)}, u32[]{:S(2)}, u32[]{:S(2)}) collective-permute-start(bf16[256,192]{1,0:T(8,128)(2,1)} %get-tuple-element.72.refs_7_), channel_id=1, source_target_pairs={{0,3},{1,2},{2,1},{3,0},{4,7},{5,6},{6,5},{7,4},{8,11},{9,10},{10,... | collective-permute-start | bytes 294920 | tf_op jit(solution)/shard_map/ppermute | solution.py:470
  114.5 40.7 %collective-permute-start.26 = (bf16[768,768]{1,0:T(8,128)(2,1)S(1)}, bf16[768,768]{1,0:T(8,128)(2,1)}, u32[]{:S(2)}, u32[]{:S(2)}) collective-permute-start(bf16[768,768]{1,0:T(8,128)(2,1)S(1)} %bitcast.45), channel_id=1, source_target_pairs={{0,1},{1,0},{2,3},{3,2},{4,5},{5,4},{6,7},{7,6},{8,9},{9,8},{10,11... | collective-permute-start | bytes 3538952 | tf_op jit(solution)/shard_map/ppermute | solution.py:470
  114.6 40.6 %collective-permute-start.25 = (bf16[768,768]{1,0:T(8,128)(2,1)}, bf16[768,768]{1,0:T(8,128)(2,1)}, u32[]{:S(2)}, u32[]{:S(2)}) collective-permute-start(bf16[768,768]{1,0:T(8,128)(2,1)} %collective-permute-done.1.refs_10_), channel_id=1, source_target_pairs={{0,1},{1,0},{2,3},{3,2},{4,5},{5,4},{6,7},{7,6},{8,9},{9,8},{10,11... | collective-permute-start | bytes 3538952 | tf_op jit(solution)/shard_map/ppermute | solution.py:470
  115.0 40.2 %collective-permute-start.28 = (bf16[768,768]{1,0:T(8,128)(2,1)}, bf16[768,768]{1,0:T(8,128)(2,1)}, u32[]{:S(2)}, u32[]{:S(2)}) collective-permute-start(bf16[768,768]{1,0:T(8,128)(2,1)} %collective-permute-done.27.refs_14_.refs_6_), channel_id=1, source_target_pairs={{0,1},{1,0},{2,3},{3,2},{4,5},{5,4},{6,7},{7,6},{8,9},{9,8},{10,11... | collective-permute-start | bytes 3538952 | tf_op jit(solution)/shard_map/ppermute | solution.py:470
  119.0 2.4 collective-permute-start.16
  120.0 34.6 %copy-start.2 = (bf16[8,64,768]{2,1,0:T(8,128)(2,1)}, bf16[8,64,768]{2,1,0:T(8,128)(2,1)S(1)}, u32[]{:S(2)}) copy-start(bf16[8,64,768]{2,1,0:T(8,128)(2,1)S(1)} %all-to-all-done) | copy-start | bytes 2359300
  126.0 5.7 %collective-permute-start.17 = (bf16[64,768]{1,0:T(8,128)(2,1)}, bf16[64,768]{1,0:T(8,128)(2,1)S(1)}, u32[]{:S(2)}, u32[]{:S(2)}) collective-permute-start(bf16[64,768]{1,0:T(8,128)(2,1)} %get-tuple-element.75), channel_id=1, source_target_pairs={{0,4},{4,0},{8,12},{12,8},{16,20},{20,16},{24,28},{28,24},{1,5},{5... | collective-permute-start | bytes 294920 | tf_op jit(solution)/shard_map/ppermute | solution.py:470
  127.6 8.6 %collective-permute-start.18 = (bf16[64,768]{1,0:T(8,128)(2,1)}, bf16[64,768]{1,0:T(8,128)(2,1)S(1)}, u32[]{:S(2)}, u32[]{:S(2)}) collective-permute-start(bf16[64,768]{1,0:T(8,128)(2,1)} %get-tuple-element.76), channel_id=1, source_target_pairs={{0,8},{4,12},{8,0},{12,4},{16,24},{20,28},{24,16},{28,20},{1,9},{5... | collective-permute-start | bytes 294920 | tf_op jit(solution)/shard_map/ppermute | solution.py:470
  131.7 8.0 %collective-permute-start.19 = (bf16[64,768]{1,0:T(8,128)(2,1)}, bf16[64,768]{1,0:T(8,128)(2,1)S(1)}, u32[]{:S(2)}, u32[]{:S(2)}) collective-permute-start(bf16[64,768]{1,0:T(8,128)(2,1)} %get-tuple-element.77), channel_id=1, source_target_pairs={{0,12},{4,8},{8,4},{12,0},{16,28},{20,24},{24,20},{28,16},{1,13},{... | collective-permute-start | bytes 294920 | tf_op jit(solution)/shard_map/ppermute | solution.py:470
  136.2 10.7 %collective-permute-start.20 = (bf16[64,768]{1,0:T(8,128)(2,1)}, bf16[64,768]{1,0:T(8,128)(2,1)S(1)}, u32[]{:S(2)}, u32[]{:S(2)}) collective-permute-start(bf16[64,768]{1,0:T(8,128)(2,1)} %get-tuple-element.78), channel_id=1, source_target_pairs={{0,16},{4,20},{8,24},{12,28},{16,0},{20,4},{24,8},{28,12},{1,17},{... | collective-permute-start | bytes 294920 | tf_op jit(solution)/shard_map/ppermute | solution.py:470
  139.7 7.5 %collective-permute-start.23 = (bf16[64,768]{1,0:T(8,128)(2,1)}, bf16[64,768]{1,0:T(8,128)(2,1)S(1)}, u32[]{:S(2)}, u32[]{:S(2)}) collective-permute-start(bf16[64,768]{1,0:T(8,128)(2,1)} %get-tuple-element.81), channel_id=1, source_target_pairs={{0,28},{4,24},{8,20},{12,16},{16,12},{20,8},{24,4},{28,0},{1,29},{... | collective-permute-start | bytes 294920 | tf_op jit(solution)/shard_map/ppermute | solution.py:470
  146.9 7.7 %collective-permute-start.21 = (bf16[64,768]{1,0:T(8,128)(2,1)}, bf16[64,768]{1,0:T(8,128)(2,1)S(1)}, u32[]{:S(2)}, u32[]{:S(2)}) collective-permute-start(bf16[64,768]{1,0:T(8,128)(2,1)} %get-tuple-element.79), channel_id=1, source_target_pairs={{0,20},{4,16},{8,28},{12,24},{16,4},{20,0},{24,12},{28,8},{1,21},{... | collective-permute-start | bytes 294920 | tf_op jit(solution)/shard_map/ppermute | solution.py:470
  147.2 8.0 %collective-permute-start.22 = (bf16[64,768]{1,0:T(8,128)(2,1)}, bf16[64,768]{1,0:T(8,128)(2,1)S(1)}, u32[]{:S(2)}, u32[]{:S(2)}) collective-permute-start(bf16[64,768]{1,0:T(8,128)(2,1)} %get-tuple-element.80), channel_id=1, source_target_pairs={{0,24},{4,28},{8,16},{12,20},{16,8},{20,12},{24,0},{28,4},{1,25},{... | collective-permute-start | bytes 294920 | tf_op jit(solution)/shard_map/ppermute | solution.py:470
  154.6 22.0 %collective-permute-start.29 = (bf16[512,768]{1,0:T(8,128)(2,1)S(1)}, bf16[512,768]{1,0:T(8,128)(2,1)S(1)}, u32[]{:S(2)}, u32[]{:S(2)}) collective-permute-start(bf16[512,768]{1,0:T(8,128)(2,1)S(1)} %bitcast.23), channel_id=1, source_target_pairs={{0,2},{1,3},{2,0},{3,1},{4,6},{5,7},{6,4},{7,5},{8,10},{9,11},{10,... | collective-permute-start | bytes 2359304 | tf_op jit(solution)/shard_map/ppermute | solution.py:470
  172.1 7.1 %collective-permute-start.30 = (bf16[64,768]{1,0:T(8,128)(2,1)}, bf16[64,768]{1,0:T(8,128)(2,1)S(1)}, u32[]{:S(2)}, u32[]{:S(2)}) collective-permute-start(bf16[64,768]{1,0:T(8,128)(2,1)} %get-tuple-element.92), channel_id=1, source_target_pairs={{0,4},{4,0},{8,12},{12,8},{16,20},{20,16},{24,28},{28,24},{1,5},{5... | collective-permute-start | bytes 294920 | tf_op jit(solution)/shard_map/ppermute | solution.py:470
  173.3 7.0 %collective-permute-start.31 = (bf16[64,768]{1,0:T(8,128)(2,1)}, bf16[64,768]{1,0:T(8,128)(2,1)S(1)}, u32[]{:S(2)}, u32[]{:S(2)}) collective-permute-start(bf16[64,768]{1,0:T(8,128)(2,1)} %get-tuple-element.93), channel_id=1, source_target_pairs={{0,8},{4,12},{8,0},{12,4},{16,24},{20,28},{24,16},{28,20},{1,9},{5... | collective-permute-start | bytes 294920 | tf_op jit(solution)/shard_map/ppermute | solution.py:470
  174.9 15.6 %collective-permute-start.32 = (bf16[64,768]{1,0:T(8,128)(2,1)}, bf16[64,768]{1,0:T(8,128)(2,1)S(1)}, u32[]{:S(2)}, u32[]{:S(2)}) collective-permute-start(bf16[64,768]{1,0:T(8,128)(2,1)} %get-tuple-element.94), channel_id=1, source_target_pairs={{0,12},{4,8},{8,4},{12,0},{16,28},{20,24},{24,20},{28,16},{1,13},{... | collective-permute-start | bytes 294920 | tf_op jit(solution)/shard_map/ppermute | solution.py:470
  175.6 14.9 %collective-permute-start.33 = (bf16[64,768]{1,0:T(8,128)(2,1)}, bf16[64,768]{1,0:T(8,128)(2,1)S(1)}, u32[]{:S(2)}, u32[]{:S(2)}) collective-permute-start(bf16[64,768]{1,0:T(8,128)(2,1)} %get-tuple-element.95), channel_id=1, source_target_pairs={{0,16},{4,20},{8,24},{12,28},{16,0},{20,4},{24,8},{28,12},{1,17},{... | collective-permute-start | bytes 294920 | tf_op jit(solution)/shard_map/ppermute | solution.py:470
  176.6 14.8 %collective-permute-start.34 = (bf16[64,768]{1,0:T(8,128)(2,1)}, bf16[64,768]{1,0:T(8,128)(2,1)S(1)}, u32[]{:S(2)}, u32[]{:S(2)}) collective-permute-start(bf16[64,768]{1,0:T(8,128)(2,1)} %get-tuple-element.96), channel_id=1, source_target_pairs={{0,20},{4,16},{8,28},{12,24},{16,4},{20,0},{24,12},{28,8},{1,21},{... | collective-permute-start | bytes 294920 | tf_op jit(solution)/shard_map/ppermute | solution.py:470
  179.1 12.3 %collective-permute-start.35 = (bf16[64,768]{1,0:T(8,128)(2,1)}, bf16[64,768]{1,0:T(8,128)(2,1)S(1)}, u32[]{:S(2)}, u32[]{:S(2)}) collective-permute-start(bf16[64,768]{1,0:T(8,128)(2,1)} %get-tuple-element.97), channel_id=1, source_target_pairs={{0,24},{4,28},{8,16},{12,20},{16,8},{20,12},{24,0},{28,4},{1,25},{... | collective-permute-start | bytes 294920 | tf_op jit(solution)/shard_map/ppermute | solution.py:470
  180.3 11.2 %collective-permute-start.36 = (bf16[64,768]{1,0:T(8,128)(2,1)}, bf16[64,768]{1,0:T(8,128)(2,1)S(1)}, u32[]{:S(2)}, u32[]{:S(2)}) collective-permute-start(bf16[64,768]{1,0:T(8,128)(2,1)} %get-tuple-element.98), channel_id=1, source_target_pairs={{0,28},{4,24},{8,20},{12,16},{16,12},{20,8},{24,4},{28,0},{1,29},{... | collective-permute-start | bytes 294920 | tf_op jit(solution)/shard_map/ppermute | solution.py:470
  195.8 8.0 %collective-permute-start.38 = (bf16[256,768]{1,0:T(8,128)(2,1)}, bf16[256,768]{1,0:T(8,128)(2,1)S(1)}, u32[]{:S(2)}, u32[]{:S(2)}) collective-permute-start(bf16[256,768]{1,0:T(8,128)(2,1)} %get-tuple-element.99.refs_8_), channel_id=1, source_target_pairs={{0,2},{1,3},{2,0},{3,1},{4,6},{5,7},{6,4},{7,5},{8,10},{9,11},{10,... | collective-permute-start | bytes 1179656 | tf_op jit(solution)/shard_map/ppermute | solution.py:470
  203.8 6.7 %collective-permute-start.39 = (bf16[256,768]{1,0:T(8,128)(2,1)S(1)}, bf16[256,768]{1,0:T(8,128)(2,1)S(1)}, u32[]{:S(2)}, u32[]{:S(2)}) collective-permute-start(bf16[256,768]{1,0:T(8,128)(2,1)S(1)} %collective-permute-done.38.refs_10_), channel_id=1, source_target_pairs={{0,1},{1,0},{2,3},{3,2},{4,5},{5,4},{6,7},{7,6},{8,9},{9,8},{10,11... | collective-permute-start | bytes 1179656 | tf_op jit(solution)/shard_map/ppermute | solution.py:470
  203.8 7.0 %collective-permute-start.37 = (bf16[256,768]{1,0:T(8,128)(2,1)}, bf16[256,768]{1,0:T(8,128)(2,1)S(1)}, u32[]{:S(2)}, u32[]{:S(2)}) collective-permute-start(bf16[256,768]{1,0:T(8,128)(2,1)} %get-tuple-element.99.refs_8_), channel_id=1, source_target_pairs={{0,1},{1,0},{2,3},{3,2},{4,5},{5,4},{6,7},{7,6},{8,9},{9,8},{10,11... | collective-permute-start | bytes 1179656 | tf_op jit(solution)/shard_map/ppermute | solution.py:470
  204.3 100.7 %all-to-all-start.1 = ((bf16[8,64,768]{2,1,0:T(8,128)(2,1)}), bf16[8,64,768]{2,1,0:T(8,128)(2,1)S(1)}, u32[]{:S(2)}, u32[]{:S(2)}) async-start(bf16[8,64,768]{2,1,0:T(8,128)(2,1)} %bitcast.14), calls=%async_computation.1 | async-start | bytes 1572864 | tf_op jit(solution)/shard_map/all_to_all | solution.py:494
  210.5 40.8 %collective-permute-start.51 = (bf16[512,768]{1,0:T(8,128)(2,1)}, bf16[512,768]{1,0:T(8,128)(2,1)}, u32[]{:S(2)}, u32[]{:S(2)}) collective-permute-start(bf16[512,768]{1,0:T(8,128)(2,1)} %get-tuple-element.119.rows_ref.refs_0_), channel_id=1, source_target_pairs={{0,2},{1,3},{2,0},{3,1},{4,6},{5,7},{6,4},{7,5},{8,10},{9,11},{10,... | collective-permute-start | bytes 2359304 | tf_op jit(solution)/shard_map/ppermute | solution.py:470
  211.6 28.9 %copy-start.3 = (bf16[8,64,768]{2,1,0:T(8,128)(2,1)S(1)}, bf16[8,64,768]{2,1,0:T(8,128)(2,1)}, u32[]{:S(2)}) copy-start(bf16[8,64,768]{2,1,0:T(8,128)(2,1)} %copy-done.2) | copy-start | bytes 2359300
  211.6 29.2 %copy-start.15 = (bf16[512,768]{1,0:T(8,128)(2,1)S(1)}, bf16[512,768]{1,0:T(8,128)(2,1)}, u32[]{:S(2)}) copy-start(bf16[512,768]{1,0:T(8,128)(2,1)} %copy-done.14) | copy-start | bytes 2359300
  238.5 2.3 collective-permute-start.40
  238.6 12.7 %collective-permute-start.41 = (bf16[272,768]{1,0:T(8,128)(2,1)}, bf16[272,768]{1,0:T(8,128)(2,1)S(1)}, u32[]{:S(2)}, u32[]{:S(2)}) collective-permute-start(bf16[272,768]{1,0:T(8,128)(2,1)} %get-tuple-element.108), channel_id=1, source_target_pairs={{0,2},{1,3},{2,0},{3,1},{4,6},{5,7},{6,4},{7,5},{8,10},{9,11},{10,... | collective-permute-start | bytes 1253384 | tf_op jit(solution)/shard_map/ppermute | solution.py:470
  240.4 19.0 %collective-permute-start.42 = (bf16[272,768]{1,0:T(8,128)(2,1)}, bf16[272,768]{1,0:T(8,128)(2,1)S(1)}, u32[]{:S(2)}, u32[]{:S(2)}) collective-permute-start(bf16[272,768]{1,0:T(8,128)(2,1)} %get-tuple-element.109), channel_id=1, source_target_pairs={{0,3},{1,2},{2,1},{3,0},{4,7},{5,6},{6,5},{7,4},{8,11},{9,10},{10,... | collective-permute-start | bytes 1253384 | tf_op jit(solution)/shard_map/ppermute | solution.py:470
  240.4 74.6 %collective-permute-start.53 = (bf16[512,768]{1,0:T(8,128)(2,1)S(1)}, bf16[512,768]{1,0:T(8,128)(2,1)}, u32[]{:S(2)}, u32[]{:S(2)}) collective-permute-start(bf16[512,768]{1,0:T(8,128)(2,1)S(1)} %bitcast.26), channel_id=1, source_target_pairs={{0,1},{1,0},{2,3},{3,2},{4,5},{5,4},{6,7},{7,6},{8,9},{9,8},{10,11... | collective-permute-start | bytes 2359304 | tf_op jit(solution)/shard_map/ppermute | solution.py:470
  240.8 74.3 %collective-permute-start.54 = (bf16[512,768]{1,0:T(8,128)(2,1)S(1)}, bf16[512,768]{1,0:T(8,128)(2,1)}, u32[]{:S(2)}, u32[]{:S(2)}) collective-permute-start(bf16[512,768]{1,0:T(8,128)(2,1)S(1)} %copy-done.15), channel_id=1, source_target_pairs={{0,1},{1,0},{2,3},{3,2},{4,5},{5,4},{6,7},{7,6},{8,9},{9,8},{10,11... | collective-permute-start | bytes 2359304 | tf_op jit(solution)/shard_map/ppermute | solution.py:470
  251.3 63.8 %collective-permute-start.50 = (bf16[512,768]{1,0:T(8,128)(2,1)}, bf16[512,768]{1,0:T(8,128)(2,1)}, u32[]{:S(2)}, u32[]{:S(2)}) collective-permute-start(bf16[512,768]{1,0:T(8,128)(2,1)} %get-tuple-element.119.rows_ref.refs_0_), channel_id=1, source_target_pairs={{0,1},{1,0},{2,3},{3,2},{4,5},{5,4},{6,7},{7,6},{8,9},{9,8},{10,11... | collective-permute-start | bytes 2359304 | tf_op jit(solution)/shard_map/ppermute | solution.py:470
  251.3 63.8 %collective-permute-start.52 = (bf16[512,768]{1,0:T(8,128)(2,1)}, bf16[512,768]{1,0:T(8,128)(2,1)}, u32[]{:S(2)}, u32[]{:S(2)}) collective-permute-start(bf16[512,768]{1,0:T(8,128)(2,1)} %collective-permute-done.51.refs_2_), channel_id=1, source_target_pairs={{0,1},{1,0},{2,3},{3,2},{4,5},{5,4},{6,7},{7,6},{8,9},{9,8},{10,11... | collective-permute-start | bytes 2359304 | tf_op jit(solution)/shard_map/ppermute | solution.py:470
  263.2 4.0 %collective-permute-start.43 = (bf16[16,768]{1,0:T(8,128)(2,1)}, bf16[16,768]{1,0:T(8,128)(2,1)S(1)}, u32[]{:S(2)}, u32[]{:S(2)}) collective-permute-start(bf16[16,768]{1,0:T(8,128)(2,1)} %get-tuple-element.111.refs_0_), channel_id=1, source_target_pairs={{0,4},{4,0},{8,12},{12,8},{16,20},{20,16},{24,28},{28,24},{1,5},{5... | collective-permute-start | bytes 73736 | tf_op jit(solution)/shard_map/ppermute | solution.py:470
  267.2 33.0 %copy-start.52 = (bf16[16,768]{1,0:T(8,128)(2,1)}, bf16[16,768]{1,0:T(8,128)(2,1)S(1)}, u32[]{:S(2)}) copy-start(bf16[16,768]{1,0:T(8,128)(2,1)S(1)} %collective-permute-done.43.refs_1_) | copy-start | bytes 73732
  267.2 4.0 %collective-permute-start.44 = (bf16[16,768]{1,0:T(8,128)(2,1)}, bf16[16,768]{1,0:T(8,128)(2,1)S(1)}, u32[]{:S(2)}, u32[]{:S(2)}) collective-permute-start(bf16[16,768]{1,0:T(8,128)(2,1)} %get-tuple-element.111.refs_0_), channel_id=1, source_target_pairs={{0,8},{4,12},{8,0},{12,4},{16,24},{20,28},{24,16},{28,20},{1,9},{5... | collective-permute-start | bytes 73736 | tf_op jit(solution)/shard_map/ppermute | solution.py:470
  271.3 29.0 %copy-start.53 = (bf16[16,768]{1,0:T(8,128)(2,1)}, bf16[16,768]{1,0:T(8,128)(2,1)S(1)}, u32[]{:S(2)}) copy-start(bf16[16,768]{1,0:T(8,128)(2,1)S(1)} %collective-permute-done.44.refs_2_) | copy-start | bytes 73732
  271.3 4.9 %collective-permute-start.45 = (bf16[16,768]{1,0:T(8,128)(2,1)}, bf16[16,768]{1,0:T(8,128)(2,1)S(1)}, u32[]{:S(2)}, u32[]{:S(2)}) collective-permute-start(bf16[16,768]{1,0:T(8,128)(2,1)} %get-tuple-element.111.refs_0_), channel_id=1, source_target_pairs={{0,12},{4,8},{8,4},{12,0},{16,28},{20,24},{24,20},{28,16},{1,13},{... | collective-permute-start | bytes 73736 | tf_op jit(solution)/shard_map/ppermute | solution.py:470
  276.2 4.9 %collective-permute-start.46 = (bf16[16,768]{1,0:T(8,128)(2,1)}, bf16[16,768]{1,0:T(8,128)(2,1)S(1)}, u32[]{:S(2)}, u32[]{:S(2)}) collective-permute-start(bf16[16,768]{1,0:T(8,128)(2,1)} %get-tuple-element.111.refs_0_), channel_id=1, source_target_pairs={{0,16},{4,20},{8,24},{12,28},{16,0},{20,4},{24,8},{28,12},{1,17},{... | collective-permute-start | bytes 73736 | tf_op jit(solution)/shard_map/ppermute | solution.py:470
  281.2 6.1 %collective-permute-start.47 = (bf16[16,768]{1,0:T(8,128)(2,1)}, bf16[16,768]{1,0:T(8,128)(2,1)S(1)}, u32[]{:S(2)}, u32[]{:S(2)}) collective-permute-start(bf16[16,768]{1,0:T(8,128)(2,1)} %get-tuple-element.111.refs_0_), channel_id=1, source_target_pairs={{0,20},{4,16},{8,28},{12,24},{16,4},{20,0},{24,12},{28,8},{1,21},{... | collective-permute-start | bytes 73736 | tf_op jit(solution)/shard_map/ppermute | solution.py:470
  287.2 6.2 %collective-permute-start.48 = (bf16[16,768]{1,0:T(8,128)(2,1)}, bf16[16,768]{1,0:T(8,128)(2,1)S(1)}, u32[]{:S(2)}, u32[]{:S(2)}) collective-permute-start(bf16[16,768]{1,0:T(8,128)(2,1)} %get-tuple-element.111.refs_0_), channel_id=1, source_target_pairs={{0,24},{4,28},{8,16},{12,20},{16,8},{20,12},{24,0},{28,4},{1,25},{... | collective-permute-start | bytes 73736 | tf_op jit(solution)/shard_map/ppermute | solution.py:470
  293.5 6.8 %collective-permute-start.49 = (bf16[16,768]{1,0:T(8,128)(2,1)}, bf16[16,768]{1,0:T(8,128)(2,1)S(1)}, u32[]{:S(2)}, u32[]{:S(2)}) collective-permute-start(bf16[16,768]{1,0:T(8,128)(2,1)} %get-tuple-element.111.refs_0_), channel_id=1, source_target_pairs={{0,28},{4,24},{8,20},{12,16},{16,12},{20,8},{24,4},{28,0},{1,29},{... | collective-permute-start | bytes 73736 | tf_op jit(solution)/shard_map/ppermute | solution.py:470
  305.9 27.1 %all-to-all-start.2 = ((bf16[8,96,768]{2,1,0:T(8,128)(2,1)}), bf16[8,96,768]{2,1,0:T(8,128)(2,1)S(1)}, u32[]{:S(2)}, u32[]{:S(2)}) async-start(bf16[8,96,768]{2,1,0:T(8,128)(2,1)} %bitcast.16), calls=%async_computation.2 | async-start | bytes 2359296 | tf_op jit(solution)/shard_map/all_to_all | solution.py:494
  (53 other events, 456.5 us)
where the time goes:
time: 342 us; the launch traced here: 336 us
  waiting for transfers between devices  125 us (37%)
  Pallas kernels  107 us (31%)
  starting transfers between devices  87.7 us (26%)
  local copies, waits for them, and re-layouts  13.3 us (4%)
    ppermute x55, waiting for transfers between devices, permuted(): return lax.ppermute(value, axis, [(i, i ^ bit) for i in range(size)])  124 us
    pallas_call x14, Pallas kernels, call(): pl.pallas_call(kernel, out_shape=tuple(outs), in_specs=[pl.BlockSpec(memo...  107 us
    ppermute x55, starting transfers between devices, permuted(): return lax.ppermute(value, axis, [(i, i ^ bit) for i in range(size)])  69.8 us
    all_to_all x3, starting transfers between devices, sent_to_all(): return lax.all_to_all(parts, axis, split_axis=0, concat_axis=0, tiled=True)  17.9 us
    unnamed x120, local copies, waits for them, and re-layouts  9.17 us
  transfers between devices with their start and end apart: 58, of which 27 were waited for; matrix products, arithmetic and copies ran while one was open for 2% of the time, Pallas kernels for 25%

commit v1 on v0

--- a/solution.py
+++ b/solution.py
@@ -16,14 +16,15 @@
 
 
 kernel_times = {
-    "attend": 15.0,
+    "attend": 4.0,
     "middle": 4.0,
     "expert": 16.0,
     "expert_value": 7.0,
-    "expert_weight_grads": 18.0,
+    "expert_weight_grads": 0.1,
+    "attn_weight_sums": 0.1,
     "middle_back": 4.0,
-    "attend_back": 27.0,
-    "mixed": 3.0,
+    "attend_back": 4.0,
+    "mixed": 0.1,
     "grad_tokens": 3.0,
 }
 
@@ -113,7 +114,8 @@
 
 def norm_kernel(tok_ref, gain_ref, out_ref):
     values = tok_ref[...].astype(f32)
-    out_ref[...] = (values * rms_scale(values) * gain_ref[...]).astype(low)
+    gain = gain_ref[...].reshape(1, values.shape[1])
+    out_ref[...] = (values * rms_scale(values) * gain).astype(low)
 
 
 def dispatch_kernel(capacity, rcol_ref, rrow_ref, cot_ref, out_ref):
@@ -451,13 +453,10 @@
     out_ref[...] = total[:, 3 * width :].T
 
 
-def small_sum_kernel(gain_ref, *refs):
-    parts, (gain_one_ref, table_ref, gain_two_ref, router_ref) = refs[:-4], refs[-4:]
-    total = parts[0][...].astype(f32)
-    for part in parts[1:]:
-        total = total + part[...].astype(f32)
-    gain_one_ref[...] = (total[0:1] + total[1:2]) / gain_ref[...]
-    gain_two_ref[...] = total[2:3] + total[3:4]
+def small_sum_kernel(gain_ref, parts_ref, gain_one_ref, table_ref, gain_two_ref, router_ref):
+    total = jnp.sum(parts_ref[...].astype(f32), axis=0)
+    gain_one_ref[...] = ((total[0:1] + total[1:2]) / gain_ref[...]).reshape(gain_one_ref.shape)
+    gain_two_ref[...] = (total[2:3] + total[3:4]).reshape(gain_two_ref.shape)
     table = total[4:5] + total[5:6]
     buckets = table_ref.shape[1]
     for h in range(table_ref.shape[0]):
@@ -470,12 +469,15 @@
     return lax.ppermute(value, axis, [(i, i ^ bit) for i in range(size)])
 
 
-def gathered(value, axis):
+def gathered(value, axis, *before_second):
     size = lax.axis_size(axis)
     held = {0: value}
     bit = size // 2
     while bit:
-        held.update({j ^ bit: permuted(held[j], axis, bit) for j in list(held)})
+        sent = list(held.items())
+        if bit < size // 2 and before_second:
+            sent = [(j, after(piece, *before_second)) for j, piece in sent]
+        held.update({j ^ bit: permuted(piece, axis, bit) for j, piece in sent})
         bit //= 2
     return [held[j] for j in range(size)]
 
@@ -547,7 +549,7 @@
 
     packed = jnp.concatenate([w_qkv[0], w_qkv[1], w_qkv[2], w_attn_out.T], axis=1)
     (normed,) = call(
-        norm_kernel, "norm_one", [like((tok_rows, model_width), low)], (tokens, gain_one)
+        norm_kernel, "norm_one", [like((tok_rows, model_width), low)], (tokens, gain_attn)
     )
     group = gathered(normed, "mp")
     ready = group[0]
@@ -583,7 +585,15 @@
         functools.partial(attend_kernel, heads),
         "attend",
         [like((3, length, width), low)] + [like((tok_rows, width), low)] * model_size,
-        (me, *group, w_heads, table, buckets, seg_col, segments),
+        (
+            me,
+            *group,
+            after(w_heads, all_in[model_size // 2]),
+            table,
+            buckets,
+            seg_col,
+            segments,
+        ),
         scratch=[
             pltpu.VMEM((length, model_width), low),
             pltpu.VMEM((heads, tok_rows, span), f32),
@@ -592,8 +602,8 @@
         smem=1,
     )
     got_contexts = exchanged(contexts, "mp")
-    all_out = gathered(after(own_out, got_contexts[model_size // 2]), "mp")
-    early_tokens = after(tokens, got_cot, all_in[model_size // 2])
+    far = model_size // 2
+    early_tokens = after(tokens, got_cot)
     mid, *send_rows = call(
         functools.partial(middle_kernel, capacity, model_size),
         "middle",
@@ -604,6 +614,8 @@
         smem=1,
     )
     got_rows = exchanged(send_rows, "dp")
+    late_out = after(own_out, got_contexts[far], out_weights[far])
+    all_out = gathered(late_out, "mp", *got_rows)
     outs = call(
         functools.partial(expert_kernel, sources, model_size),
         "expert",
@@ -630,8 +642,8 @@
         (expert, rows, router_rows, *hidden, *all_out),
         smem=1,
     )
-    all_cot = gathered(after(got_cot, got_rows[-1]), "mp")
-    back_grad[0] = after(back_grad[0], value_slots, all_cot[model_size // 2])
+    all_cot = gathered(after(got_cot, got_rows[-1]), "mp", rows)
+    back_grad[0] = after(back_grad[0], value_slots, *all_cot[1:])
     grad_mid, grad_low, grad_gain_moe = call(
         functools.partial(middle_back_kernel, capacity),
         "middle_back",
@@ -645,7 +657,6 @@
         smem=1,
     )
     grad_group = gathered(grad_low, "mp")
-    all_rows = gathered(after(rows, grad_group[-1]), "mp")
     back_value = sent_to_all(value_slots.reshape(slot_shape), "dp").reshape(slots, model_width)
     grad_weight_part, *grad_parts = call(
         functools.partial(attend_back_kernel, heads),
@@ -677,6 +688,7 @@
         ],
         smem=1,
     )
+    all_rows = gathered(after(rows, grad_group[far]), "mp", grad_weight_part)
     got_parts = exchanged(grad_parts, "mp")
     got_weights = sent_to_all(
         grad_weight_part.reshape(data_size, weight_rows, 4 * width), "dp"
@@ -702,43 +714,40 @@
         functools.partial(mixed_kernel, capacity),
         "mixed",
         [like((tok_rows, model_width), low)],
-        (routes, route_row, after(back_value, grad_weight_part), mid),
+        (routes, route_row, after(back_value, grad_expert_in), mid),
     )
     grad_tokens, small = call(
         functools.partial(last_kernel, expert_count),
         "grad_tokens",
         [like((tok_rows, model_width), f32), like((small_count, model_width), low)],
-        (tokens, gain_one, grad_mid, *got_parts),
-    )
-    if sources == 1:
-        smalls = [jnp.sum(repeated(small, "dp").astype(f32), axis=0)]
-    else:
-        smalls = exchanged([small] * data_size, "dp")
+        (tokens, gain_one, after(grad_mid, grad_expert_in), *got_parts),
+    )
+    smalls = repeated(small, "dp")
     grad_attn_out, grad_qkv = call(
         weight_sum_kernel,
         "attn_weight_sums",
         [like((width, weight_rows), f32), like((3, weight_rows, width), f32)],
-        (got_weights,),
+        (after(got_weights, grad_expert_in),),
     )
     grad_gain_attn, grad_table, sum_gain_moe, grad_router = call(
         small_sum_kernel,
         "small_sums",
         [
-            like((1, model_width), f32),
+            like((model_width,), f32),
             like((total_heads, bucket_count), f32),
-            like((1, model_width), f32),
+            like((model_width,), f32),
             like((expert_count, model_width), f32),
         ],
-        (gain_one, *smalls),
+        (gain_one, smalls),
     )
     return (
         mixed,
         grad_tokens,
-        grad_gain_attn.reshape(model_width),
+        grad_gain_attn,
         grad_qkv,
         grad_attn_out,
         grad_table,
-        sum_gain_moe.reshape(model_width),
+        sum_gain_moe,
         grad_router.T,
         grad_expert_in[None],
         grad_expert_out[None],

time: 342 us -> 309 us (0.904)
  waiting for transfers between devices: 125 us -> 96.1 us
  starting transfers between devices: 87.7 us -> 70.3 us
  blocking collectives: 0 us -> 14.2 us
    ppermute x55 -> x48, waiting for transfers between devices: 124 us -> 72.5 us  [permuted(): return lax.ppermute(value, axis, [(i, i ^ bit) for i in range(size)])]
    all_to_all x3, waiting for transfers between devices: 0.63 us -> 23.6 us  [sent_to_all(): return lax.all_to_all(parts, axis, split_axis=0, concat_axis=0, tiled=True)]
    ppermute x55 -> x48, starting transfers between devices: 69.8 us -> 53.9 us  [permuted(): return lax.ppermute(value, axis, [(i, i ^ bit) for i in range(size)])]
    all_to_all x0 -> x1, blocking collectives: none -> 14.2 us  [sent_to_all(): return lax.all_to_all(parts, axis, split_axis=0, concat_axis=0, tiled=True)]
    unnamed x120 -> x114, local copies, waits for them, and re-layouts: 9.17 us -> 9.45 us
  transfers between devices with their start and end apart: 58 -> 51, of which waited for: 27 -> 15; matrix products, arithmetic and copies ran while one was open for 2% -> 1% of each run, Pallas kernels for 25% -> 33%
where the time goes in v1:
time: 309 us; the launch traced here: 303 us
  Pallas kernels  107 us (35%)
  waiting for transfers between devices  96.1 us (31%)
  starting transfers between devices  70.3 us (23%)
  blocking collectives  14.2 us (5%)
  local copies, waits for them, and re-layouts  13.6 us (4%)
    pallas_call x14, Pallas kernels, call(): pl.pallas_call(kernel, out_shape=tuple(outs), in_specs=[pl.BlockSpec(memo...  107 us
    ppermute x48, waiting for transfers between devices, permuted(): return lax.ppermute(value, axis, [(i, i ^ bit) for i in range(size)])  72.5 us
    ppermute x48, starting transfers between devices, permuted(): return lax.ppermute(value, axis, [(i, i ^ bit) for i in range(size)])  53.9 us
    all_to_all x3, waiting for transfers between devices, sent_to_all(): return lax.all_to_all(parts, axis, split_axis=0, concat_axis=0, tiled=True)  23.6 us
    all_to_all x3, starting transfers between devices, sent_to_all(): return lax.all_to_all(parts, axis, split_axis=0, concat_axis=0, tiled=True)  16.4 us
    all_to_all x1, blocking collectives, sent_to_all(): return lax.all_to_all(parts, axis, split_axis=0, concat_axis=0, tiled=True)  14.2 us
    unnamed x114, local copies, waits for them, and re-layouts  9.45 us
  transfers between devices with their start and end apart: 51, of which 15 were waited for; matrix products, arithmetic and copies ran while one was open for 1% of the time, Pallas kernels for 33%

profile of v1, /device:TPU:0, one launch (start us, length us, event | category | flops | bytes accessed | tf_op | source)
XLA Modules:
  0.0 303.2 jit_solution(4474949188895275833)
XLA Ops:
  0.7 3.0 collective-permute-start.10
  3.7 1.9 norm_one.1.refs_0_
  5.9 4.2 %collective-permute-start = (bf16[96,768]{1,0:T(8,128)(2,1)S(1)}, bf16[96,768]{1,0:T(8,128)(2,1)S(1)}, u32[]{:S(2)}, u32[]{:S(2)}) collective-permute-start(bf16[96,768]{1,0:T(8,128)(2,1)S(1)} %pad_maximum_fusion.refs_0_), channel_id=1, source_target_pairs={{0,24},{4,28},{8,16},{12,20},{16,8},{20,12},{24,0},{28,4},{1,25},{... | collective-permute-start | bytes 442376 | tf_op jit(solution)/shard_map/ppermute | solution.py:469
  10.7 4.1 %collective-permute-done.refs_6_ = bf16[96,768]{1,0:T(8,128)(2,1)S(1)} collective-permute-done((bf16[96,768]{1,0:T(8,128)(2,1)S(1)}, bf16[96,768]{1,0:T(8,128)(2,1)S(1)}, u32[]{:S(2)}, u32[]{:S(2)}) %collective-permute-start) | collective-permute-done | bytes 147488 | tf_op jit(solution)/shard_map/ppermute | solution.py:469
  14.8 1.8 collective-permute-start.4
  16.6 0.9 collective-permute-done.5.refs_2_
  17.4 1.5 collective-permute-start.9
  18.9 1.0 copy.30.refs_7_.refs_16_
  20.0 0.8 copy.34.rcol_ref
  20.8 1.2 collective-permute-done.7.refs_4_
  22.0 1.6 collective-permute-start.6
  23.6 1.3 collective-permute-start.8
  24.9 13.4 %collective-permute-done.2.refs_2_ = bf16[256,768]{1,0:T(8,128)(2,1)S(1)} collective-permute-done((bf16[256,768]{1,0:T(8,128)(2,1)}, bf16[256,768]{1,0:T(8,128)(2,1)S(1)}, u32[]{:S(2)}, u32[]{:S(2)}) %collective-permute-start.2) | collective-permute-done | bytes 393248 | tf_op jit(solution)/shard_map/ppermute | solution.py:469
  38.3 2.6 dispatch_cotangent.1
  40.9 6.1 %all-to-all-start = ((bf16[8,64,768]{2,1,0:T(8,128)(2,1)}), bf16[8,64,768]{2,1,0:T(8,128)(2,1)}, u32[]{:S(2)}, u32[]{:S(2)}) async-start(bf16[8,64,768]{2,1,0:T(8,128)(2,1)} %bitcast.33), calls=%async_computation | async-start | bytes 1572864 | tf_op jit(solution)/shard_map/all_to_all | solution.py:496
  48.3 2.7 attn_weights.1
  50.9 1.5 collective-permute-start.15
  52.4 0.8 copy-done.32
  53.3 14.9 %attend.1 = (bf16[3,1024,192]{2,1,0:T(8,128)(2,1)}, bf16[256,192]{1,0:T(8,128)(2,1)}, bf16[256,192]{1,0:T(8,128)(2,1)}, bf16[256,192]{1,0:T(8,128)(2,1)}, bf16[256,192]{1,0:T(8,128)(2,1)}) custom-call(s32[1]{0:T(128)} %bitcast.9.me_ref, bf16[256,768]{1,0:T(8,128)(2,1)} %norm_one.1.refs_0_, bf16[256,768]{1,0:T(8,128)(2,1)} %copy-done.31, ...), custom_call_target="tpu_custom_call" | custom-call | flops 4600000000 | tf_op jit(solution)/shard_map/attend/pallas_call | solution.py:45
  68.8 4.9 %collective-permute-done.12.refs_2_ = bf16[256,192]{1,0:T(8,128)(2,1)S(1)} collective-permute-done((bf16[256,192]{1,0:T(8,128)(2,1)}, bf16[256,192]{1,0:T(8,128)(2,1)S(1)}, u32[]{:S(2)}, u32[]{:S(2)}) %collective-permute-start.12) | collective-permute-done | bytes 98336 | tf_op jit(solution)/shard_map/ppermute | solution.py:469
  73.6 0.7 copy-done.41
  75.3 1.6 collective-permute-start.13
  77.6 24.4 %collective-permute-done.13.refs_3_ = bf16[256,192]{1,0:T(8,128)(2,1)} collective-permute-done((bf16[256,192]{1,0:T(8,128)(2,1)}, bf16[256,192]{1,0:T(8,128)(2,1)}, u32[]{:S(2)}, u32[]{:S(2)}) %collective-permute-start.13) | collective-permute-done | bytes 98336 | tf_op jit(solution)/shard_map/ppermute | solution.py:469
  102.1 3.9 %middle.1 = (f32[256,768]{1,0:T(8,128)}, bf16[64,768]{1,0:T(8,128)(2,1)}, bf16[64,768]{1,0:T(8,128)(2,1)}, bf16[64,768]{1,0:T(8,128)(2,1)}, bf16[64,768]{1,0:T(8...) custom-call(s32[1]{0:T(128)} %bitcast.1.me_ref, ...), custom_call_target="tpu_custom_call" | custom-call | flops 4600000000 | tf_op jit(solution)/shard_map/middle/pallas_call | solution.py:45
  105.9 1.3 collective-permute-start.17
  107.2 1.5 collective-permute-start.18
  108.7 0.8 collective-permute-start.19
  109.5 2.1 collective-permute-start.20
  111.6 2.5 collective-permute-start.21
  114.1 2.2 collective-permute-start.22
  116.3 1.4 collective-permute-done.19.refs_3_
  117.8 2.6 collective-permute-start.23
  120.7 7.0 %collective-permute-done.21.refs_5_ = bf16[64,768]{1,0:T(8,128)(2,1)S(1)} collective-permute-done((bf16[64,768]{1,0:T(8,128)(2,1)}, bf16[64,768]{1,0:T(8,128)(2,1)S(1)}, u32[]{:S(2)}, u32[]{:S(2)}) %collective-permute-start.21) | collective-permute-done | bytes 98336 | tf_op jit(solution)/shard_map/ppermute | solution.py:469
  129.6 0.9 collective-permute-start.30
  130.5 1.7 collective-permute-done.26.refs_13_.refs_5_
  132.2 1.7 collective-permute-done.28.refs_15_.refs_7_
  134.0 1.0 copy-done.23
  134.9 16.0 %expert.1 = (bf16[64,768]{1,0:T(8,128)(2,1)}, bf16[64,768]{1,0:T(8,128)(2,1)}, bf16[64,768]{1,0:T(8,128)(2,1)}, bf16[64,768]{1,0:T(8,128)(2,1)}, bf16[64,768]{1,...) custom-call(s32[1]{0:T(128)} %bitcast.1.me_ref, ...), custom_call_target="tpu_custom_call" | custom-call | flops 18400000000 | tf_op jit(solution)/shard_map/expert/pallas_call | solution.py:45
  151.6 1.2 collective-permute-start.32
  152.7 3.6 %collective-permute-start.33 = (bf16[64,768]{1,0:T(8,128)(2,1)}, bf16[64,768]{1,0:T(8,128)(2,1)S(1)}, u32[]{:S(2)}, u32[]{:S(2)}) collective-permute-start(bf16[64,768]{1,0:T(8,128)(2,1)} %get-tuple-element.107), channel_id=1, source_target_pairs={{0,8},{4,12},{8,0},{12,4},{16,24},{20,28},{24,16},{28,20},{1,9},{5... | collective-permute-start | bytes 294920 | tf_op jit(solution)/shard_map/ppermute | solution.py:469
  156.6 5.2 %collective-permute-start.35 = (bf16[64,768]{1,0:T(8,128)(2,1)}, bf16[64,768]{1,0:T(8,128)(2,1)S(1)}, u32[]{:S(2)}, u32[]{:S(2)}) collective-permute-start(bf16[64,768]{1,0:T(8,128)(2,1)} %get-tuple-element.109), channel_id=1, source_target_pairs={{0,16},{4,20},{8,24},{12,28},{16,0},{20,4},{24,8},{28,12},{1,17},{... | collective-permute-start | bytes 294920 | tf_op jit(solution)/shard_map/ppermute | solution.py:469
  161.9 2.3 collective-permute-start.36
  164.7 3.3 %collective-permute-start.38 = (bf16[64,768]{1,0:T(8,128)(2,1)}, bf16[64,768]{1,0:T(8,128)(2,1)S(1)}, u32[]{:S(2)}, u32[]{:S(2)}) collective-permute-start(bf16[64,768]{1,0:T(8,128)(2,1)} %get-tuple-element.112), channel_id=1, source_target_pairs={{0,28},{4,24},{8,20},{12,16},{16,12},{20,8},{24,4},{28,0},{1,29},{... | collective-permute-start | bytes 294920 | tf_op jit(solution)/shard_map/ppermute | solution.py:469
  168.0 7.2 %expert_value.1 = bf16[512,768]{1,0:T(8,128)(2,1)} custom-call(s32[1]{0:T(128)} %bitcast.1.me_ref, bf16[512,768]{1,0:T(8,128)(2,1)} %get-tuple-element.120.rows_ref.refs_0_, bf16[8,768]{1,0:T(8,128)(2,1)} %bitcast.36, bf16[512,768]{1,0:T(8,128)(2,1)} %get-tuple-element.96.refs_0_, bf16[512,768]{1,0:T(8,128)(2,1)} %get-tuple-element.97.refs_1_, ...), custom_call_target="tpu_custom_call" | custom-call | flops 8049999872 | tf_op jit(solution)/shard_map/expert_value/pallas_call | solution.py:45
  176.0 3.6 %middle_back.1 = (f32[256,768]{1,0:T(8,128)}, bf16[256,768]{1,0:T(8,128)(2,1)}, f32[1,768]{1,0:T(1,128)}) custom-call(s32[1]{0:T(128)} %bitcast.1.me_ref, s32[256,1]{1,0:T(8,128)} %copy.34.rcol_ref, s32[1,256]{1,0:T(1,128)} %bitcast.43, f32[256,768]{1,0:T(8,128)} %get-tuple-element.100.mid_ref, bf16[256,768]{1,0:T(8,128)(2,1)} %cot_ref.2, ...), custom_call_target="tpu_custom_call" | custom-call | flops 4600000000 | tf_op jit(solution)/shard_map/middle_back/pallas_call | solution.py:45
  180.1 10.5 %collective-permute-done.40.refs_10_ = bf16[256,768]{1,0:T(8,128)(2,1)S(1)} collective-permute-done((bf16[256,768]{1,0:T(8,128)(2,1)}, bf16[256,768]{1,0:T(8,128)(2,1)S(1)}, u32[]{:S(2)}, u32[]{:S(2)}) %collective-permute-start.40) | collective-permute-done | bytes 393248 | tf_op jit(solution)/shard_map/ppermute | solution.py:469
  190.6 0.7 collective-permute-start.43
  191.4 6.7 %all-to-all-start.1 = ((bf16[8,64,768]{2,1,0:T(8,128)(2,1)}), bf16[8,64,768]{2,1,0:T(8,128)(2,1)S(1)}, u32[]{:S(2)}, u32[]{:S(2)}) async-start(bf16[8,64,768]{2,1,0:T(8,128)(2,1)} %bitcast.14), calls=%async_computation.1 | async-start | bytes 1572864 | tf_op jit(solution)/shard_map/all_to_all | solution.py:496
  198.1 0.7 copy-done.34
  199.0 27.3 %attend_back.1 = (bf16[768,768]{1,0:T(8,128)(2,1)}, bf16[272,768]{1,0:T(8,128)(2,1)}, bf16[272,768]{1,0:T(8,128)(2,1)}, bf16[272,768]{1,0:T(8,128)(2,1)}, bf16[272,768]{1,0:T(8,128)(2,1)}) custom-call(s32[1]{0:T(128)} %bitcast.9.me_ref, bf16[256,768]{1,0:T(8,128)(2,1)} %norm_one.1.refs_0_, bf16[256,768]{1,0:T(8,128)(2,1)} %copy-done.31, ...), custom_call_target="tpu_custom_call" | custom-call | flops 4600000000 | tf_op jit(solution)/shard_map/attend_back/pallas_call | solution.py:45
  226.9 1.3 collective-permute-start.46
  229.3 1.0 collective-permute-done.44.refs_3_
  230.3 0.9 copy-done.11
  231.3 17.5 %expert_weight_grads.1 = (f32[768,768]{1,0:T(8,128)}, f32[768,768]{1,0:T(8,128)}) custom-call(s32[1]{0:T(128)} %bitcast.1.me_ref, bf16[8,768]{1,0:T(8,128)(2,1)} %bitcast.37, bf16[768,768]{1,0:T(8,128)(2,1)} %bitcast.26, bf16[768,768]{1,0:T(8,128)(2,1)} %bitcast.30, bf16[512,768]{1,0:T(8,128)(2,1)} %get-tuple-element.120.rows_ref.refs_0_, ...), custom_call_target="tpu_custom_call" | custom-call | flops 115000000 | tf_op jit(solution)/shard_map/expert_weight_grads/pallas_call | solution.py:45
  248.8 0.7 copy-done.26
  249.9 3.1 %grad_tokens.1 = (f32[256,768]{1,0:T(8,128)}, bf16[16,768]{1,0:T(8,128)(2,1)}) custom-call(bf16[256,768]{1,0:T(8,128)(2,1)} %tok_ref.4, f32[1,768]{1,0:T(1,128)} %reshape.66.gain_ref, f32[256,768]{1,0:T(8,128)} %get-tuple-element.125.grad_mid_ref, bf16[272,768]{1,0:T(8,128)(2,1)} %get-tuple-element.126.refs_0_, bf16[272,768]{1,0:T(8,128)(2,1)} %copy-done.26, ...), custom_call_target="tpu_custom_call" | custom-call | flops 3449999872 | tf_op jit(solution)/shard_map/grad_tokens/pallas_call | solution.py:45
  253.0 0.8 broadcast_in_dim.9
  253.8 14.2 %all_to_all.20.parts_ref = bf16[8,16,768]{2,1,0:T(8,128)(2,1)} all-to-all(bf16[8,16,768]{2,1,0:T(8,128)(2,1)S(1)} %broadcast_in_dim.9), channel_id=1, replica_groups=mesh['dp'=8,'mp'=4] {'dp'}, dimensions={0} | all-to-all | bytes 393216 | tf_op jit(solution)/shard_map/all_to_all | solution.py:496
  268.0 3.6 %all-to-all-start.3 = ((bf16[8,96,768]{2,1,0:T(8,128)(2,1)}), bf16[8,96,768]{2,1,0:T(8,128)(2,1)S(1)}, u32[]{:S(2)}, u32[]{:S(2)}) async-start(bf16[8,96,768]{2,1,0:T(8,128)(2,1)} %bitcast.16), calls=%async_computation.3 | async-start | bytes 2359296 | tf_op jit(solution)/shard_map/all_to_all | solution.py:496
  271.6 2.9 mixed.1
  274.5 1.6 small_sums.1
  276.1 23.6 %all-to-all-done.3.parts_ref = bf16[8,96,768]{2,1,0:T(8,128)(2,1)S(1)} async-done(((bf16[8,96,768]{2,1,0:T(8,128)(2,1)}), bf16[8,96,768]{2,1,0:T(8,128)(2,1)S(1)}, u32[]{:S(2)}, u32[]{:S(2)}) %all-to-all-start.3) | async-done | bytes 1179680 | tf_op jit(solution)/shard_map/all_to_all | solution.py:496
  299.7 1.0 copy-done.1
  300.8 2.2 attn_weight_sums.1
  (176 shorter events, 11.8 us)
Async XLA Ops:
  0.6 46.4 %copy-start = (f32[12,32]{1,0:T(8,128)S(1)}, f32[12,32]{1,0:T(8,128)}, u32[]{:S(2)}) copy-start(f32[12,32]{1,0:T(8,128)} %param.18) | copy-start | bytes 4612
  0.7 51.7 %collective-permute-start.10 = (bf16[768,768]{1,0:T(8,128)(2,1)}, bf16[768,768]{1,0:T(8,128)(2,1)S(1)}, u32[]{:S(2)}, u32[]{:S(2)}) collective-permute-start(bf16[768,768]{1,0:T(8,128)(2,1)} %bitcast.24), channel_id=1, source_target_pairs={{0,2},{1,3},{2,0},{3,1},{4,6},{5,7},{6,4},{7,5},{8,10},{9,11},{10,... | collective-permute-start | bytes 3538952 | tf_op jit(solution)/shard_map/ppermute | solution.py:469
  5.6 32.7 %collective-permute-start.2 = (bf16[256,768]{1,0:T(8,128)(2,1)}, bf16[256,768]{1,0:T(8,128)(2,1)S(1)}, u32[]{:S(2)}, u32[]{:S(2)}) collective-permute-start(bf16[256,768]{1,0:T(8,128)(2,1)} %norm_one.1.refs_0_), channel_id=1, source_target_pairs={{0,2},{1,3},{2,0},{3,1},{4,6},{5,7},{6,4},{7,5},{8,10},{9,11},{10,... | collective-permute-start | bytes 1179656 | tf_op jit(solution)/shard_map/ppermute | solution.py:469
  5.9 35.0 %copy-start.13 = (bf16[96,768]{1,0:T(8,128)(2,1)}, bf16[96,768]{1,0:T(8,128)(2,1)S(1)}, u32[]{:S(2)}) copy-start(bf16[96,768]{1,0:T(8,128)(2,1)S(1)} %pad_maximum_fusion.refs_0_) | copy-start | bytes 442372
  5.9 8.9 %collective-permute-start = (bf16[96,768]{1,0:T(8,128)(2,1)S(1)}, bf16[96,768]{1,0:T(8,128)(2,1)S(1)}, u32[]{:S(2)}, u32[]{:S(2)}) collective-permute-start(bf16[96,768]{1,0:T(8,128)(2,1)S(1)} %pad_maximum_fusion.refs_0_), channel_id=1, source_target_pairs={{0,24},{4,28},{8,16},{12,20},{16,8},{20,12},{24,0},{28,4},{1,25},{... | collective-permute-start | bytes 442376 | tf_op jit(solution)/shard_map/ppermute | solution.py:469
  10.1 7.4 %collective-permute-start.5 = (bf16[96,768]{1,0:T(8,128)(2,1)S(1)}, bf16[96,768]{1,0:T(8,128)(2,1)S(1)}, u32[]{:S(2)}, u32[]{:S(2)}) collective-permute-start(bf16[96,768]{1,0:T(8,128)(2,1)S(1)} %pad_maximum_fusion.refs_0_), channel_id=1, source_target_pairs={{0,8},{4,12},{8,0},{12,4},{16,24},{20,28},{24,16},{28,20},{1,9},{5... | collective-permute-start | bytes 442376 | tf_op jit(solution)/shard_map/ppermute | solution.py:469
  10.1 11.9 %collective-permute-start.7 = (bf16[96,768]{1,0:T(8,128)(2,1)S(1)}, bf16[96,768]{1,0:T(8,128)(2,1)S(1)}, u32[]{:S(2)}, u32[]{:S(2)}) collective-permute-start(bf16[96,768]{1,0:T(8,128)(2,1)S(1)} %pad_maximum_fusion.refs_0_), channel_id=1, source_target_pairs={{0,16},{4,20},{8,24},{12,28},{16,0},{20,4},{24,8},{28,12},{1,17},{... | collective-permute-start | bytes 442376 | tf_op jit(solution)/shard_map/ppermute | solution.py:469
  14.8 26.0 %copy-start.36 = (bf16[96,768]{1,0:T(8,128)(2,1)}, bf16[96,768]{1,0:T(8,128)(2,1)S(1)}, u32[]{:S(2)}) copy-start(bf16[96,768]{1,0:T(8,128)(2,1)S(1)} %collective-permute-done.refs_6_) | copy-start | bytes 442372
  14.8 7.2 %collective-permute-start.4 = (bf16[96,768]{1,0:T(8,128)(2,1)S(1)}, bf16[96,768]{1,0:T(8,128)(2,1)S(1)}, u32[]{:S(2)}, u32[]{:S(2)}) collective-permute-start(bf16[96,768]{1,0:T(8,128)(2,1)S(1)} %pad_maximum_fusion.refs_0_), channel_id=1, source_target_pairs={{0,4},{4,0},{8,12},{12,8},{16,20},{20,16},{24,28},{28,24},{1,5},{5... | collective-permute-start | bytes 442376 | tf_op jit(solution)/shard_map/ppermute | solution.py:469
  17.4 23.4 %copy-start.37 = (bf16[96,768]{1,0:T(8,128)(2,1)}, bf16[96,768]{1,0:T(8,128)(2,1)S(1)}, u32[]{:S(2)}) copy-start(bf16[96,768]{1,0:T(8,128)(2,1)S(1)} %collective-permute-done.5.refs_2_) | copy-start | bytes 442372
  17.4 6.2 %collective-permute-start.9 = (bf16[96,768]{1,0:T(8,128)(2,1)S(1)}, bf16[96,768]{1,0:T(8,128)(2,1)S(1)}, u32[]{:S(2)}, u32[]{:S(2)}) collective-permute-start(bf16[96,768]{1,0:T(8,128)(2,1)S(1)} %collective-permute-done.refs_6_), channel_id=1, source_target_pairs={{0,4},{4,0},{8,12},{12,8},{16,20},{20,16},{24,28},{28,24},{1,5},{5... | collective-permute-start | bytes 442376 | tf_op jit(solution)/shard_map/ppermute | solution.py:469
  22.0 18.9 %copy-start.38 = (bf16[96,768]{1,0:T(8,128)(2,1)}, bf16[96,768]{1,0:T(8,128)(2,1)S(1)}, u32[]{:S(2)}) copy-start(bf16[96,768]{1,0:T(8,128)(2,1)S(1)} %collective-permute-done.7.refs_4_) | copy-start | bytes 442372
  22.0 30.4 %collective-permute-start.1 = (bf16[256,768]{1,0:T(8,128)(2,1)S(1)}, bf16[256,768]{1,0:T(8,128)(2,1)S(1)}, u32[]{:S(2)}, u32[]{:S(2)}) collective-permute-start(bf16[256,768]{1,0:T(8,128)(2,1)S(1)} %copy-done.29), channel_id=1, source_target_pairs={{0,1},{1,0},{2,3},{3,2},{4,5},{5,4},{6,7},{7,6},{8,9},{9,8},{10,11... | collective-permute-start | bytes 1179656 | tf_op jit(solution)/shard_map/ppermute | solution.py:469
  22.0 18.9 %copy-start.39 = (bf16[96,768]{1,0:T(8,128)(2,1)}, bf16[96,768]{1,0:T(8,128)(2,1)S(1)}, u32[]{:S(2)}) copy-start(bf16[96,768]{1,0:T(8,128)(2,1)S(1)} %collective-permute-done.4.refs_1_) | copy-start | bytes 442372
  22.0 26.2 %collective-permute-start.6 = (bf16[96,768]{1,0:T(8,128)(2,1)S(1)}, bf16[96,768]{1,0:T(8,128)(2,1)}, u32[]{:S(2)}, u32[]{:S(2)}) collective-permute-start(bf16[96,768]{1,0:T(8,128)(2,1)S(1)} %collective-permute-done.5.refs_2_), channel_id=1, source_target_pairs={{0,4},{4,0},{8,12},{12,8},{16,20},{20,16},{24,28},{28,24},{1,5},{5... | collective-permute-start | bytes 442376 | tf_op jit(solution)/shard_map/ppermute | solution.py:469
  23.6 24.6 %collective-permute-start.8 = (bf16[96,768]{1,0:T(8,128)(2,1)S(1)}, bf16[96,768]{1,0:T(8,128)(2,1)}, u32[]{:S(2)}, u32[]{:S(2)}) collective-permute-start(bf16[96,768]{1,0:T(8,128)(2,1)S(1)} %collective-permute-done.7.refs_4_), channel_id=1, source_target_pairs={{0,4},{4,0},{8,12},{12,8},{16,20},{20,16},{24,28},{28,24},{1,5},{5... | collective-permute-start | bytes 442376 | tf_op jit(solution)/shard_map/ppermute | solution.py:469
  38.3 14.1 %collective-permute-start.3 = (bf16[256,768]{1,0:T(8,128)(2,1)S(1)}, bf16[256,768]{1,0:T(8,128)(2,1)S(1)}, u32[]{:S(2)}, u32[]{:S(2)}) collective-permute-start(bf16[256,768]{1,0:T(8,128)(2,1)S(1)} %collective-permute-done.2.refs_2_), channel_id=1, source_target_pairs={{0,1},{1,0},{2,3},{3,2},{4,5},{5,4},{6,7},{7,6},{8,9},{9,8},{10,11... | collective-permute-start | bytes 1179656 | tf_op jit(solution)/shard_map/ppermute | solution.py:469
  40.9 36.6 %all-to-all-start = ((bf16[8,64,768]{2,1,0:T(8,128)(2,1)}), bf16[8,64,768]{2,1,0:T(8,128)(2,1)}, u32[]{:S(2)}, u32[]{:S(2)}) async-start(bf16[8,64,768]{2,1,0:T(8,128)(2,1)} %bitcast.33), calls=%async_computation | async-start | bytes 1572864 | tf_op jit(solution)/shard_map/all_to_all | solution.py:496
  50.9 17.9 %collective-permute-start.15 = (bf16[768,192]{1,0:T(8,128)(2,1)}, bf16[768,192]{1,0:T(8,128)(2,1)}, u32[]{:S(2)}, u32[]{:S(2)}) collective-permute-start(bf16[768,192]{1,0:T(8,128)(2,1)} %get-tuple-element.83.refs_4_.refs_13_), channel_id=1, source_target_pairs={{0,2},{1,3},{2,0},{3,1},{4,6},{5,7},{6,4},{7,5},{8,10},{9,11},{10,... | collective-permute-start | bytes 884744 | tf_op jit(solution)/shard_map/ppermute | solution.py:469
  52.4 75.3 %copy-start.20 = (bf16[768,768]{1,0:T(8,128)(2,1)}, bf16[768,768]{1,0:T(8,128)(2,1)S(1)}, u32[]{:S(2)}) copy-start(bf16[768,768]{1,0:T(8,128)(2,1)S(1)} %collective-permute-done.10.refs_10_) | copy-start | bytes 3538948
  53.3 21.0 %copy-start.4 = (bf16[1,768,768]{2,1,0:T(8,128)(2,1)S(1)}, bf16[1,768,768]{2,1,0:T(8,128)(2,1)}, u32[]{:S(2)}) copy-start(bf16[1,768,768]{2,1,0:T(8,128)(2,1)} %param.25) | copy-start | bytes 3538948
  53.3 23.6 %copy-start.18 = (f32[768]{0:T(1024)S(1)}, f32[768]{0:T(1024)}, u32[]{:S(2)}) copy-start(f32[768]{0:T(1024)} %param.21) | copy-start | bytes 9220
  68.2 5.4 %collective-permute-start.12 = (bf16[256,192]{1,0:T(8,128)(2,1)}, bf16[256,192]{1,0:T(8,128)(2,1)S(1)}, u32[]{:S(2)}, u32[]{:S(2)}) collective-permute-start(bf16[256,192]{1,0:T(8,128)(2,1)} %get-tuple-element.81.refs_6_), channel_id=1, source_target_pairs={{0,2},{1,3},{2,0},{3,1},{4,6},{5,7},{6,4},{7,5},{8,10},{9,11},{10,... | collective-permute-start | bytes 294920 | tf_op jit(solution)/shard_map/ppermute | solution.py:469
  74.3 55.2 %collective-permute-start.27 = (bf16[768,768]{1,0:T(8,128)(2,1)S(1)}, bf16[768,768]{1,0:T(8,128)(2,1)S(1)}, u32[]{:S(2)}, u32[]{:S(2)}) collective-permute-start(bf16[768,768]{1,0:T(8,128)(2,1)S(1)} %bitcast.31), channel_id=1, source_target_pairs={{0,2},{1,3},{2,0},{3,1},{4,6},{5,7},{6,4},{7,5},{8,10},{9,11},{10,... | collective-permute-start | bytes 3538952 | tf_op jit(solution)/shard_map/ppermute | solution.py:469
  74.8 2.7 collective-permute-start.14
  74.8 2.7 collective-permute-start.16
  75.3 2.3 collective-permute-start.11
  75.3 26.7 %collective-permute-start.13 = (bf16[256,192]{1,0:T(8,128)(2,1)}, bf16[256,192]{1,0:T(8,128)(2,1)}, u32[]{:S(2)}, u32[]{:S(2)}) collective-permute-start(bf16[256,192]{1,0:T(8,128)(2,1)} %get-tuple-element.82.refs_7_), channel_id=1, source_target_pairs={{0,3},{1,2},{2,1},{3,0},{4,7},{5,6},{6,5},{7,4},{8,11},{9,10},{10,... | collective-permute-start | bytes 294920 | tf_op jit(solution)/shard_map/ppermute | solution.py:469
  105.9 5.6 %collective-permute-start.17 = (bf16[64,768]{1,0:T(8,128)(2,1)}, bf16[64,768]{1,0:T(8,128)(2,1)S(1)}, u32[]{:S(2)}, u32[]{:S(2)}) collective-permute-start(bf16[64,768]{1,0:T(8,128)(2,1)} %get-tuple-element.85), channel_id=1, source_target_pairs={{0,4},{4,0},{8,12},{12,8},{16,20},{20,16},{24,28},{28,24},{1,5},{5... | collective-permute-start | bytes 294920 | tf_op jit(solution)/shard_map/ppermute | solution.py:469
  107.2 6.9 %collective-permute-start.18 = (bf16[64,768]{1,0:T(8,128)(2,1)}, bf16[64,768]{1,0:T(8,128)(2,1)S(1)}, u32[]{:S(2)}, u32[]{:S(2)}) collective-permute-start(bf16[64,768]{1,0:T(8,128)(2,1)} %get-tuple-element.86), channel_id=1, source_target_pairs={{0,8},{4,12},{8,0},{12,4},{16,24},{20,28},{24,16},{28,20},{1,9},{5... | collective-permute-start | bytes 294920 | tf_op jit(solution)/shard_map/ppermute | solution.py:469
  108.7 9.1 %collective-permute-start.19 = (bf16[64,768]{1,0:T(8,128)(2,1)}, bf16[64,768]{1,0:T(8,128)(2,1)S(1)}, u32[]{:S(2)}, u32[]{:S(2)}) collective-permute-start(bf16[64,768]{1,0:T(8,128)(2,1)} %get-tuple-element.87), channel_id=1, source_target_pairs={{0,12},{4,8},{8,4},{12,0},{16,28},{20,24},{24,20},{28,16},{1,13},{... | collective-permute-start | bytes 294920 | tf_op jit(solution)/shard_map/ppermute | solution.py:469
  109.5 10.9 %collective-permute-start.20 = (bf16[64,768]{1,0:T(8,128)(2,1)}, bf16[64,768]{1,0:T(8,128)(2,1)S(1)}, u32[]{:S(2)}, u32[]{:S(2)}) collective-permute-start(bf16[64,768]{1,0:T(8,128)(2,1)} %get-tuple-element.88), channel_id=1, source_target_pairs={{0,16},{4,20},{8,24},{12,28},{16,0},{20,4},{24,8},{28,12},{1,17},{... | collective-permute-start | bytes 294920 | tf_op jit(solution)/shard_map/ppermute | solution.py:469
  111.6 22.3 %copy-start.42 = (bf16[64,768]{1,0:T(8,128)(2,1)}, bf16[64,768]{1,0:T(8,128)(2,1)S(1)}, u32[]{:S(2)}) copy-start(bf16[64,768]{1,0:T(8,128)(2,1)S(1)} %collective-permute-done.17.refs_1_) | copy-start | bytes 294916
  111.6 16.1 %collective-permute-start.21 = (bf16[64,768]{1,0:T(8,128)(2,1)}, bf16[64,768]{1,0:T(8,128)(2,1)S(1)}, u32[]{:S(2)}, u32[]{:S(2)}) collective-permute-start(bf16[64,768]{1,0:T(8,128)(2,1)} %get-tuple-element.89), channel_id=1, source_target_pairs={{0,20},{4,16},{8,28},{12,24},{16,4},{20,0},{24,12},{28,8},{1,21},{... | collective-permute-start | bytes 294920 | tf_op jit(solution)/shard_map/ppermute | solution.py:469
  114.1 19.8 %copy-start.43 = (bf16[64,768]{1,0:T(8,128)(2,1)}, bf16[64,768]{1,0:T(8,128)(2,1)S(1)}, u32[]{:S(2)}) copy-start(bf16[64,768]{1,0:T(8,128)(2,1)S(1)} %collective-permute-done.18.refs_2_) | copy-start | bytes 294916
  114.1 13.6 %collective-permute-start.22 = (bf16[64,768]{1,0:T(8,128)(2,1)}, bf16[64,768]{1,0:T(8,128)(2,1)S(1)}, u32[]{:S(2)}, u32[]{:S(2)}) collective-permute-start(bf16[64,768]{1,0:T(8,128)(2,1)} %get-tuple-element.90), channel_id=1, source_target_pairs={{0,24},{4,28},{8,16},{12,20},{16,8},{20,12},{24,0},{28,4},{1,25},{... | collective-permute-start | bytes 294920 | tf_op jit(solution)/shard_map/ppermute | solution.py:469
  117.8 10.0 %collective-permute-start.23 = (bf16[64,768]{1,0:T(8,128)(2,1)}, bf16[64,768]{1,0:T(8,128)(2,1)S(1)}, u32[]{:S(2)}, u32[]{:S(2)}) collective-permute-start(bf16[64,768]{1,0:T(8,128)(2,1)} %get-tuple-element.91), channel_id=1, source_target_pairs={{0,28},{4,24},{8,20},{12,16},{16,12},{20,8},{24,4},{28,0},{1,29},{... | collective-permute-start | bytes 294920 | tf_op jit(solution)/shard_map/ppermute | solution.py:469
  120.4 10.2 %collective-permute-start.24 = (bf16[768,768]{1,0:T(8,128)(2,1)S(1)}, bf16[768,768]{1,0:T(8,128)(2,1)S(1)}, u32[]{:S(2)}, u32[]{:S(2)}) collective-permute-start(bf16[768,768]{1,0:T(8,128)(2,1)S(1)} %bitcast.27), channel_id=1, source_target_pairs={{0,1},{1,0},{2,3},{3,2},{4,5},{5,4},{6,7},{7,6},{8,9},{9,8},{10,11... | collective-permute-start | bytes 3538952 | tf_op jit(solution)/shard_map/ppermute | solution.py:469
  127.7 2.8 collective-permute-start.25
  129.0 3.2 %collective-permute-start.26 = (bf16[768,768]{1,0:T(8,128)(2,1)S(1)}, bf16[768,768]{1,0:T(8,128)(2,1)S(1)}, u32[]{:S(2)}, u32[]{:S(2)}) collective-permute-start(bf16[768,768]{1,0:T(8,128)(2,1)S(1)} %bitcast.32), channel_id=1, source_target_pairs={{0,1},{1,0},{2,3},{3,2},{4,5},{5,4},{6,7},{7,6},{8,9},{9,8},{10,11... | collective-permute-start | bytes 3538952 | tf_op jit(solution)/shard_map/ppermute | solution.py:469
  129.5 4.4 %collective-permute-start.28 = (bf16[768,768]{1,0:T(8,128)(2,1)S(1)}, bf16[768,768]{1,0:T(8,128)(2,1)S(1)}, u32[]{:S(2)}, u32[]{:S(2)}) collective-permute-start(bf16[768,768]{1,0:T(8,128)(2,1)S(1)} %collective-permute-done.27.refs_14_.refs_6_), channel_id=1, source_target_pairs={{0,1},{1,0},{2,3},{3,2},{4,5},{5,4},{6,7},{7,6},{8,9},{9,8},{10,11... | collective-permute-start | bytes 3538952 | tf_op jit(solution)/shard_map/ppermute | solution.py:469
  129.6 21.4 %collective-permute-start.30 = (bf16[512,768]{1,0:T(8,128)(2,1)}, bf16[512,768]{1,0:T(8,128)(2,1)S(1)}, u32[]{:S(2)}, u32[]{:S(2)}) collective-permute-start(bf16[512,768]{1,0:T(8,128)(2,1)} %bitcast.7.cot_ref.refs_4_), channel_id=1, source_target_pairs={{0,2},{1,3},{2,0},{3,1},{4,6},{5,7},{6,4},{7,5},{8,10},{9,11},{10,... | collective-permute-start | bytes 2359304 | tf_op jit(solution)/shard_map/ppermute | solution.py:469
  151.0 24.2 %copy-start.5 = (bf16[512,768]{1,0:T(8,128)(2,1)}, bf16[512,768]{1,0:T(8,128)(2,1)S(1)}, u32[]{:S(2)}) copy-start(bf16[512,768]{1,0:T(8,128)(2,1)S(1)} %collective-permute-done.30.refs_6_) | copy-start | bytes 2359300
  151.0 13.2 %collective-permute-start.31 = (bf16[512,768]{1,0:T(8,128)(2,1)S(1)}, bf16[512,768]{1,0:T(8,128)(2,1)S(1)}, u32[]{:S(2)}, u32[]{:S(2)}) collective-permute-start(bf16[512,768]{1,0:T(8,128)(2,1)S(1)} %collective-permute-done.30.refs_6_), channel_id=1, source_target_pairs={{0,1},{1,0},{2,3},{3,2},{4,5},{5,4},{6,7},{7,6},{8,9},{9,8},{10,11... | collective-permute-start | bytes 2359304 | tf_op jit(solution)/shard_map/ppermute | solution.py:469
  151.2 13.5 %collective-permute-start.29 = (bf16[512,768]{1,0:T(8,128)(2,1)}, bf16[512,768]{1,0:T(8,128)(2,1)S(1)}, u32[]{:S(2)}, u32[]{:S(2)}) collective-permute-start(bf16[512,768]{1,0:T(8,128)(2,1)} %bitcast.7.cot_ref.refs_4_), channel_id=1, source_target_pairs={{0,1},{1,0},{2,3},{3,2},{4,5},{5,4},{6,7},{7,6},{8,9},{9,8},{10,11... | collective-permute-start | bytes 2359304 | tf_op jit(solution)/shard_map/ppermute | solution.py:469
  151.6 5.0 %collective-permute-start.32 = (bf16[64,768]{1,0:T(8,128)(2,1)}, bf16[64,768]{1,0:T(8,128)(2,1)S(1)}, u32[]{:S(2)}, u32[]{:S(2)}) collective-permute-start(bf16[64,768]{1,0:T(8,128)(2,1)} %get-tuple-element.106), channel_id=1, source_target_pairs={{0,4},{4,0},{8,12},{12,8},{16,20},{20,16},{24,28},{28,24},{1,5},{5... | collective-permute-start | bytes 294920 | tf_op jit(solution)/shard_map/ppermute | solution.py:469
  152.7 9.1 %collective-permute-start.33 = (bf16[64,768]{1,0:T(8,128)(2,1)}, bf16[64,768]{1,0:T(8,128)(2,1)S(1)}, u32[]{:S(2)}, u32[]{:S(2)}) collective-permute-start(bf16[64,768]{1,0:T(8,128)(2,1)} %get-tuple-element.107), channel_id=1, source_target_pairs={{0,8},{4,12},{8,0},{12,4},{16,24},{20,28},{24,16},{28,20},{1,9},{5... | collective-permute-start | bytes 294920 | tf_op jit(solution)/shard_map/ppermute | solution.py:469
  156.3 18.9 %collective-permute-start.34 = (bf16[64,768]{1,0:T(8,128)(2,1)}, bf16[64,768]{1,0:T(8,128)(2,1)S(1)}, u32[]{:S(2)}, u32[]{:S(2)}) collective-permute-start(bf16[64,768]{1,0:T(8,128)(2,1)} %get-tuple-element.108), channel_id=1, source_target_pairs={{0,12},{4,8},{8,4},{12,0},{16,28},{20,24},{24,20},{28,16},{1,13},{... | collective-permute-start | bytes 294920 | tf_op jit(solution)/shard_map/ppermute | solution.py:469
  156.6 18.6 %collective-permute-start.35 = (bf16[64,768]{1,0:T(8,128)(2,1)}, bf16[64,768]{1,0:T(8,128)(2,1)S(1)}, u32[]{:S(2)}, u32[]{:S(2)}) collective-permute-start(bf16[64,768]{1,0:T(8,128)(2,1)} %get-tuple-element.109), channel_id=1, source_target_pairs={{0,16},{4,20},{8,24},{12,28},{16,0},{20,4},{24,8},{28,12},{1,17},{... | collective-permute-start | bytes 294920 | tf_op jit(solution)/shard_map/ppermute | solution.py:469
  161.9 13.4 %collective-permute-start.36 = (bf16[64,768]{1,0:T(8,128)(2,1)}, bf16[64,768]{1,0:T(8,128)(2,1)S(1)}, u32[]{:S(2)}, u32[]{:S(2)}) collective-permute-start(bf16[64,768]{1,0:T(8,128)(2,1)} %get-tuple-element.110), channel_id=1, source_target_pairs={{0,20},{4,16},{8,28},{12,24},{16,4},{20,0},{24,12},{28,8},{1,21},{... | collective-permute-start | bytes 294920 | tf_op jit(solution)/shard_map/ppermute | solution.py:469
  164.2 11.1 %collective-permute-start.37 = (bf16[64,768]{1,0:T(8,128)(2,1)}, bf16[64,768]{1,0:T(8,128)(2,1)S(1)}, u32[]{:S(2)}, u32[]{:S(2)}) collective-permute-start(bf16[64,768]{1,0:T(8,128)(2,1)} %get-tuple-element.111), channel_id=1, source_target_pairs={{0,24},{4,28},{8,16},{12,20},{16,8},{20,12},{24,0},{28,4},{1,25},{... | collective-permute-start | bytes 294920 | tf_op jit(solution)/shard_map/ppermute | solution.py:469
  164.7 10.6 %collective-permute-start.38 = (bf16[64,768]{1,0:T(8,128)(2,1)}, bf16[64,768]{1,0:T(8,128)(2,1)S(1)}, u32[]{:S(2)}, u32[]{:S(2)}) collective-permute-start(bf16[64,768]{1,0:T(8,128)(2,1)} %get-tuple-element.112), channel_id=1, source_target_pairs={{0,28},{4,24},{8,20},{12,16},{16,12},{20,8},{24,4},{28,0},{1,29},{... | collective-permute-start | bytes 294920 | tf_op jit(solution)/shard_map/ppermute | solution.py:469
  179.6 11.1 %collective-permute-start.40 = (bf16[256,768]{1,0:T(8,128)(2,1)}, bf16[256,768]{1,0:T(8,128)(2,1)S(1)}, u32[]{:S(2)}, u32[]{:S(2)}) collective-permute-start(bf16[256,768]{1,0:T(8,128)(2,1)} %get-tuple-element.113.refs_8_), channel_id=1, source_target_pairs={{0,2},{1,3},{2,0},{3,1},{4,6},{5,7},{6,4},{7,5},{8,10},{9,11},{10,... | collective-permute-start | bytes 1179656 | tf_op jit(solution)/shard_map/ppermute | solution.py:469
  180.1 18.0 %collective-permute-start.39 = (bf16[256,768]{1,0:T(8,128)(2,1)}, bf16[256,768]{1,0:T(8,128)(2,1)S(1)}, u32[]{:S(2)}, u32[]{:S(2)}) collective-permute-start(bf16[256,768]{1,0:T(8,128)(2,1)} %get-tuple-element.113.refs_8_), channel_id=1, source_target_pairs={{0,1},{1,0},{2,3},{3,2},{4,5},{5,4},{6,7},{7,6},{8,9},{9,8},{10,11... | collective-permute-start | bytes 1179656 | tf_op jit(solution)/shard_map/ppermute | solution.py:469
  190.6 7.4 %collective-permute-start.41 = (bf16[256,768]{1,0:T(8,128)(2,1)S(1)}, bf16[256,768]{1,0:T(8,128)(2,1)S(1)}, u32[]{:S(2)}, u32[]{:S(2)}) collective-permute-start(bf16[256,768]{1,0:T(8,128)(2,1)S(1)} %collective-permute-done.40.refs_10_), channel_id=1, source_target_pairs={{0,1},{1,0},{2,3},{3,2},{4,5},{5,4},{6,7},{7,6},{8,9},{9,8},{10,11... | collective-permute-start | bytes 1179656 | tf_op jit(solution)/shard_map/ppermute | solution.py:469
  190.6 35.7 %collective-permute-start.43 = (bf16[512,768]{1,0:T(8,128)(2,1)S(1)}, bf16[512,768]{1,0:T(8,128)(2,1)S(1)}, u32[]{:S(2)}, u32[]{:S(2)}) collective-permute-start(bf16[512,768]{1,0:T(8,128)(2,1)S(1)} %copy-done.6), channel_id=1, source_target_pairs={{0,2},{1,3},{2,0},{3,1},{4,6},{5,7},{6,4},{7,5},{8,10},{9,11},{10,... | collective-permute-start | bytes 2359304 | tf_op jit(solution)/shard_map/ppermute | solution.py:469
  191.4 61.6 %all-to-all-start.1 = ((bf16[8,64,768]{2,1,0:T(8,128)(2,1)}), bf16[8,64,768]{2,1,0:T(8,128)(2,1)S(1)}, u32[]{:S(2)}, u32[]{:S(2)}) async-start(bf16[8,64,768]{2,1,0:T(8,128)(2,1)} %bitcast.14), calls=%async_computation.1 | async-start | bytes 1572864 | tf_op jit(solution)/shard_map/all_to_all | solution.py:496
  199.0 29.8 %copy-start.19 = (f32[768]{0:T(1024)S(1)}, f32[768]{0:T(1024)}, u32[]{:S(2)}) copy-start(f32[768]{0:T(1024)} %gain_ref.1) | copy-start | bytes 9220
  226.3 3.0 %collective-permute-start.42 = (bf16[512,768]{1,0:T(8,128)(2,1)S(1)}, bf16[512,768]{1,0:T(8,128)(2,1)S(1)}, u32[]{:S(2)}, u32[]{:S(2)}) collective-permute-start(bf16[512,768]{1,0:T(8,128)(2,1)S(1)} %copy-done.6), channel_id=1, source_target_pairs={{0,1},{1,0},{2,3},{3,2},{4,5},{5,4},{6,7},{7,6},{8,9},{9,8},{10,11... | collective-permute-start | bytes 2359304 | tf_op jit(solution)/shard_map/ppermute | solution.py:469
  226.4 4.0 %collective-permute-start.44 = (bf16[512,768]{1,0:T(8,128)(2,1)S(1)}, bf16[512,768]{1,0:T(8,128)(2,1)S(1)}, u32[]{:S(2)}, u32[]{:S(2)}) collective-permute-start(bf16[512,768]{1,0:T(8,128)(2,1)S(1)} %collective-permute-done.43.refs_2_), channel_id=1, source_target_pairs={{0,1},{1,0},{2,3},{3,2},{4,5},{5,4},{6,7},{7,6},{8,9},{9,8},{10,11... | collective-permute-start | bytes 2359304 | tf_op jit(solution)/shard_map/ppermute | solution.py:469
  226.8 21.9 %collective-permute-start.45 = (bf16[272,768]{1,0:T(8,128)(2,1)}, bf16[272,768]{1,0:T(8,128)(2,1)S(1)}, u32[]{:S(2)}, u32[]{:S(2)}) collective-permute-start(bf16[272,768]{1,0:T(8,128)(2,1)} %get-tuple-element.127), channel_id=1, source_target_pairs={{0,1},{1,0},{2,3},{3,2},{4,5},{5,4},{6,7},{7,6},{8,9},{9,8},{10,11... | collective-permute-start | bytes 1253384 | tf_op jit(solution)/shard_map/ppermute | solution.py:469
  226.9 21.8 %collective-permute-start.46 = (bf16[272,768]{1,0:T(8,128)(2,1)}, bf16[272,768]{1,0:T(8,128)(2,1)S(1)}, u32[]{:S(2)}, u32[]{:S(2)}) collective-permute-start(bf16[272,768]{1,0:T(8,128)(2,1)} %get-tuple-element.128), channel_id=1, source_target_pairs={{0,2},{1,3},{2,0},{3,1},{4,6},{5,7},{6,4},{7,5},{8,10},{9,11},{10,... | collective-permute-start | bytes 1253384 | tf_op jit(solution)/shard_map/ppermute | solution.py:469
  228.2 20.6 %collective-permute-start.47 = (bf16[272,768]{1,0:T(8,128)(2,1)}, bf16[272,768]{1,0:T(8,128)(2,1)S(1)}, u32[]{:S(2)}, u32[]{:S(2)}) collective-permute-start(bf16[272,768]{1,0:T(8,128)(2,1)} %get-tuple-element.129), channel_id=1, source_target_pairs={{0,3},{1,2},{2,1},{3,0},{4,7},{5,6},{6,5},{7,4},{8,11},{9,10},{10,... | collective-permute-start | bytes 1253384 | tf_op jit(solution)/shard_map/ppermute | solution.py:469
  268.0 31.7 %all-to-all-start.3 = ((bf16[8,96,768]{2,1,0:T(8,128)(2,1)}), bf16[8,96,768]{2,1,0:T(8,128)(2,1)S(1)}, u32[]{:S(2)}, u32[]{:S(2)}) async-start(bf16[8,96,768]{2,1,0:T(8,128)(2,1)} %bitcast.16), calls=%async_computation.3 | async-start | bytes 2359296 | tf_op jit(solution)/shard_map/all_to_all | solution.py:496
  (43 other events, 241.3 us)
